TPU v7x, 512 devices: a whole 4x8x8 slice. The times are simulated.
512 devices in a mesh: ctx: 32 (over x, z), ch: 8 (over y), rep: 2 (over core).
Axes of the slice: x: 4, y: 8, z: 8, core: 2. Of those that a mesh axis runs over, the one named last changes fastest.
Arguments:
- projections: bfloat16 [3, 8192, 8192], P(None, 'ctx', ('ch', 'rep')), may hold values from -6 to 6
- short_taps: float32 [3, 3, 8192], P(None, None, ('ch', 'rep')), may hold values from -3 to 3
- skip_gain: float32 [8192], P(('ch', 'rep')), may hold values from 0.5 to 1.5
- long_filter: float32 [8192, 8192], P('ctx', ('ch', 'rep')), may hold values from -3 to 3
- request_ends: int32 [128], replicated, may hold values from 1 to 8191, as said below
- replica_of: int32 [128], replicated, may hold values from 0 to 31, as said below
- slot_index: int32 [128], replicated, may hold values from 0 to 3, as said below
Outputs:
- output: bfloat16 [8192, 8192], P('ctx', ('ch', 'rep'))
- states: bfloat16 [128, 7, 8192], P('ctx')
Inputs may be any that keep to these rules, and one draw needn't show every extreme that they name: `request_ends`: every end lies at least one token past the start of its block of 256 tokens; at most 16 ends fall in one such block, and some block holds exactly 16. `replica_of`: each replica receives exactly 4 requests. The pairs (replica_of, slot_index) are all distinct, so every slot is filled once.
All inputs are finite; a program needn't handle non-finite values.
Results may differ from a plain program's by a relative error of at most 0.001.
Values may be sent and summed in bfloat16 or wider, within the bound.
A program may use at most 64 MiB of HBM per device.

v0:
```python
import math

import jax
import jax.numpy as jnp
from jax import lax
from jax.sharding import PartitionSpec as P

SLOTS = 4


highest = lax.Precision.HIGHEST


def passed_along(shard, axis, by):
    size = lax.axis_size(axis)
    pairs = [(i, i + by) for i in range(size) if 0 <= i + by < size]
    return lax.ppermute(shard, axis, pairs)


def angle_table(first, second, modulus):
    product = first[:, None] * second[None, :] % modulus
    angles = 2.0 * math.pi / modulus * product.astype(jnp.float32)
    return (jnp.cos(angles), jnp.sin(angles))


def short_conv(projections, short_taps):
    block_rows = projections.shape[1]
    tail_rows = passed_along(projections[:, block_rows - 2 :, :], "ctx", 1)
    extended = jnp.concatenate([tail_rows, projections], axis=1).astype(jnp.float32)
    return (
        short_taps[:, 0, None, :] * extended[:, 2:]
        + short_taps[:, 1, None, :] * extended[:, 1 : block_rows + 1]
        + short_taps[:, 2, None, :] * extended[:, :block_rows]
    )


def forward_local(spread, my_index):
    ctx_count = spread.shape[1]
    sub_rows = spread.shape[2]
    full_len = 2 * ctx_count * ctx_count * sub_rows
    span = jnp.arange(ctx_count, dtype=jnp.int32)
    twice = jnp.arange(2 * ctx_count, dtype=jnp.int32)
    cos_a, sin_a = angle_table(span, twice, 2 * ctx_count)
    real_part = jnp.einsum("ak,sajc->skjc", cos_a, spread, precision=highest)
    imag_part = -jnp.einsum("ak,sajc->skjc", sin_a, spread, precision=highest)
    positions = my_index * sub_rows + jnp.arange(sub_rows, dtype=jnp.int32)
    cos_t, sin_t = angle_table(twice, positions, full_len)
    cos_t = cos_t[None, :, :, None]
    sin_t = sin_t[None, :, :, None]
    turned_re = real_part * cos_t + imag_part * sin_t
    turned_im = imag_part * cos_t - real_part * sin_t
    return jnp.stack([turned_re, turned_im], axis=1)


def forward_finish(gathered):
    block_rows = gathered.shape[3]
    span = jnp.arange(block_rows, dtype=jnp.int32)
    cos_b, sin_b = angle_table(span, span, block_rows)
    turned_re = gathered[:, 0]
    turned_im = gathered[:, 1]
    spec_re = jnp.einsum("kb,smbc->smkc", cos_b, turned_re, precision=highest) + jnp.einsum(
        "kb,smbc->smkc", sin_b, turned_im, precision=highest
    )
    spec_im = jnp.einsum("kb,smbc->smkc", cos_b, turned_im, precision=highest) - jnp.einsum(
        "kb,smbc->smkc", sin_b, turned_re, precision=highest
    )
    return (spec_re, spec_im)


def body(projections, short_taps, skip_gain, long_filter, request_ends, replica_of, slot_index):
    block_rows = projections.shape[1]
    ctx_count = lax.axis_size("ctx")
    my_index = lax.axis_index("ctx")
    sub_rows = block_rows // ctx_count
    full_len = 2 * ctx_count * block_rows
    conv = short_conv(projections, short_taps)
    signal = conv[1] * conv[2]
    stacked = jnp.stack([signal, long_filter])[:, None]
    spread = lax.all_to_all(stacked, "ctx", split_axis=2, concat_axis=1, tiled=True)
    gathered = lax.all_to_all(
        forward_local(spread, my_index), "ctx", split_axis=2, concat_axis=3, tiled=True
    )
    spec_re, spec_im = forward_finish(gathered)
    prod_re = spec_re[0] * spec_re[1] - spec_im[0] * spec_im[1]
    prod_im = spec_re[0] * spec_im[1] + spec_im[0] * spec_re[1]
    span = jnp.arange(block_rows, dtype=jnp.int32)
    cos_b, sin_b = angle_table(span, span, block_rows)
    back_re = jnp.einsum("kb,mkc->mbc", cos_b, prod_re, precision=highest) - jnp.einsum(
        "kb,mkc->mbc", sin_b, prod_im, precision=highest
    )
    back_im = jnp.einsum("kb,mkc->mbc", cos_b, prod_im, precision=highest) + jnp.einsum(
        "kb,mkc->mbc", sin_b, prod_re, precision=highest
    )
    regrouped = lax.all_to_all(
        jnp.stack([back_re, back_im]), "ctx", split_axis=2, concat_axis=1, tiled=True
    )
    twice = jnp.arange(2 * ctx_count, dtype=jnp.int32)
    positions = my_index * sub_rows + jnp.arange(sub_rows, dtype=jnp.int32)
    cos_t, sin_t = angle_table(twice, positions, full_len)
    cos_t = cos_t[:, :, None]
    sin_t = sin_t[:, :, None]
    unturn_re = regrouped[0] * cos_t - regrouped[1] * sin_t
    unturn_im = regrouped[1] * cos_t + regrouped[0] * sin_t
    cos_a, sin_a = angle_table(twice, jnp.arange(ctx_count, dtype=jnp.int32), 2 * ctx_count)
    block_vals = (
        jnp.einsum("ka,kjc->ajc", cos_a, unturn_re, precision=highest)
        - jnp.einsum("ka,kjc->ajc", sin_a, unturn_im, precision=highest)
    ) / full_len
    mixed = lax.all_to_all(block_vals, "ctx", split_axis=0, concat_axis=1, tiled=True)[0]
    output = (conv[0] * (mixed + skip_gain[None, :] * signal)).astype(jnp.bfloat16)
    owner_dev = request_ends // block_rows
    is_mine = owner_dev == my_index
    row_index = jnp.clip(request_ends - my_index * block_rows, 1, block_rows - 1)
    prev_rows = projections[:, row_index - 1]
    cur_rows = projections[:, row_index]
    pieces = jnp.stack(
        [
            prev_rows[0],
            cur_rows[0],
            prev_rows[1],
            cur_rows[1],
            prev_rows[2],
            cur_rows[2],
            output[row_index],
        ],
        axis=1,
    )
    pieces = jnp.where(is_mine[:, None, None], pieces, jnp.zeros_like(pieces))
    target = replica_of * SLOTS + slot_index
    onehot = (target[None, :] == jnp.arange(ctx_count * SLOTS, dtype=jnp.int32)[:, None]).astype(
        jnp.float32
    )
    placed = jnp.einsum("tr,rkc->tkc", onehot, pieces.astype(jnp.float32), precision=highest)
    my_states = lax.psum_scatter(
        placed.astype(jnp.bfloat16), "ctx", scatter_dimension=0, tiled=True
    )
    states = lax.all_gather(my_states, ("ch", "rep"), axis=2, tiled=True)
    return (output, states)


def solution(mesh):
    return jax.shard_map(
        body,
        mesh=mesh,
        in_specs=(
            P(None, "ctx", ("ch", "rep")),
            P(None, None, ("ch", "rep")),
            P(("ch", "rep")),
            P("ctx", ("ch", "rep")),
            P(),
            P(),
            P(),
        ),
        out_specs=(P("ctx", ("ch", "rep")), P("ctx", None, None)),
        check_vma=False,
    )
```

profile of v0, /device:TPU:1, one launch (start us, length us, event | category | flops | bytes accessed | tf_op | source)
XLA Modules:
  0.0 475.2 jit_solution(10229278365541587391)
XLA Ops:
  7.2 0.8 slice.81
  7.9 4.8 %collective-permute-start = (bf16[3,2,512]{2,1,0:T(2,128)(2,1)S(1)}, bf16[3,2,512]{2,1,0:T(2,128)(2,1)S(1)}, u32[]{:S(2)}, u32[]{:S(2)}) collective-permute-start(bf16[3,2,512]{2,1,0:T(2,128)(2,1)S(1)} %slice.81), channel_id=1, source_target_pairs={{0,16},{16,32},{32,48},{48,64},{64,80},{80,96},{96,112},{112,128},... | collective-permute-start | bytes 18440 | tf_op jit(solution)/shard_map/ppermute | solution.py:17
  12.8 0.9 fusion.150
  13.7 1.4 maximum_convert_fusion
  15.1 0.5 fusion.8
  15.5 0.1 slice_multiply_fusion.3
  15.6 0.5 copy-done.2
  16.1 0.1 maximum_bitcast_fusion
  16.2 1.8 copy.48
  18.0 13.5 %all-to-all-start = ((f32[2,1,256,512]{3,0,1,2:T(2,128)}), f32[2,1,256,512]{3,0,1,2:T(2,128)S(1)}, u32[]{:S(2)}, u32[]{:S(2)}) async-start(f32[2,1,256,512]{3,0,1,2:T(2,128)} %copy.48), calls=%async_computation | async-start | bytes 2097152 | tf_op jit(solution)/shard_map/all_to_all | solution.py:79
  31.5 0.1 fusion.98
  31.7 24.3 %all-to-all-done = f32[2,1,256,512]{3,0,1,2:T(2,128)S(1)} async-done(((f32[2,1,256,512]{3,0,1,2:T(2,128)}), f32[2,1,256,512]{3,0,1,2:T(2,128)S(1)}, u32[]{:S(2)}, u32[]{:S(2)}) %all-to-all-start) | async-done | bytes 1048608 | tf_op jit(solution)/shard_map/all_to_all | solution.py:79
  55.9 0.2 copy.96
  56.1 2.6 fusion.24
  58.7 3.2 fusion.1
  61.9 0.7 pad_maximum_fusion
  62.6 2.4 copy.52
  65.1 99.9 %all_to_all.54 = f32[2,2,64,8,512]{4,3,0,1,2:T(8,128)S(1)} all-to-all(f32[2,2,64,8,512]{4,3,0,1,2:T(8,128)S(1)} %copy.52), channel_id=1, replica_groups=mesh['ctx'=32,'ch'=8,'rep'=2] {'ctx'}, dimensions={2} | all-to-all | bytes 8388608 | tf_op jit(solution)/shard_map/all_to_all | solution.py:80
  165.0 0.6 copy.94
  165.6 4.4 fusion.5
  170.0 4.4 fusion.4
  174.4 4.9 %add_bitcast_fusion = f32[2,2,256,512]{2,3,1,0:T(8,128)S(1)} fusion(f32[2,2,512,256]{3,2,1,0:T(8,128)S(1)} %fusion.5, f32[2,2,2,256,512]{4,3,2,1,0:T(8,128)S(1)} %bitcast.188), kind=kOutput, calls=%fused_computation.18 | convolution fusion | flops 1612054528 | bytes 6291456 | tf_op jit(solution)/shard_map/kb,smbc->smkc/dot_general | solution.py:61
  179.3 4.3 subtract_bitcast_fusion
  183.7 0.3 multiply_subtract_fusion
  183.9 2.0 fusion.19
  185.9 2.0 fusion.15
  187.9 2.2 fusion.11
  190.0 2.0 fusion.10
  192.0 1.5 pad_maximum_fusion.1
  193.5 4.2 copy.57
  197.6 8.4 %all-to-all-start.2 = ((f32[2,2,256,512]{3,1,0,2:T(2,128)}), f32[2,2,256,512]{3,1,0,2:T(2,128)}, u32[]{:S(2)}, u32[]{:S(2)}) async-start(f32[2,2,256,512]{3,1,0,2:T(2,128)} %copy.57), calls=%async_computation.2 | async-start | bytes 4194304 | tf_op jit(solution)/shard_map/all_to_all | solution.py:94
  206.1 0.1 copy.60
  206.2 0.1 copy.62
  206.3 1.8 gather_fusion.1
  208.2 1.8 gather_fusion
  210.1 0.7 fusion.53
  210.7 0.7 fusion.52
  211.4 44.1 %all-to-all-done.2 = f32[2,2,256,512]{3,1,0,2:T(2,128)} async-done(((f32[2,2,256,512]{3,1,0,2:T(2,128)}), f32[2,2,256,512]{3,1,0,2:T(2,128)}, u32[]{:S(2)}, u32[]{:S(2)}) %all-to-all-start.2) | async-done | bytes 2097184 | tf_op jit(solution)/shard_map/all_to_all | solution.py:94
  255.5 2.3 copy.95
  257.7 0.2 fusion.149
  257.9 0.1 copy.59
  258.0 0.1 copy.61
  258.1 0.3 fusion.14
  258.4 1.3 fusion.22
  259.7 1.3 fusion.12
  261.0 1.1 copy.65
  262.1 6.1 %all-to-all-start.3 = ((f32[32,8,512]{2,1,0:T(8,128)}), f32[32,8,512]{2,1,0:T(8,128)S(1)}, u32[]{:S(2)}, u32[]{:S(2)}) async-start(f32[32,8,512]{2,1,0:T(8,128)} %copy.65), calls=%async_computation.3 | async-start | bytes 1048576 | tf_op jit(solution)/shard_map/all_to_all | solution.py:109
  268.2 0.0 all-reduce.3.cloned.1.call-start
  268.3 0.7 fusion.51
  268.9 0.7 fusion.50
  269.6 0.7 fusion.49
  270.3 0.7 fusion.48
  271.0 11.0 %all-to-all-done.3 = f32[32,8,512]{2,1,0:T(8,128)S(1)} async-done(((f32[32,8,512]{2,1,0:T(8,128)}), f32[32,8,512]{2,1,0:T(8,128)S(1)}, u32[]{:S(2)}, u32[]{:S(2)}) %all-to-all-start.3) | async-done | bytes 524320 | tf_op jit(solution)/shard_map/all_to_all | solution.py:109
  282.0 0.2 fusion.31
  282.2 0.0 copy-start.1
  282.2 0.8 gather_fusion.2
  283.1 0.7 bitcast_dynamic-update-slice_fusion
  283.7 2.6 convolution_convert_fusion
  286.3 0.0 all-reduce.3.cloned.1.call-update
  286.4 1.3 dynamic-slice
  288.3 155.0 %all-reduce.3.cloned.1.call-done = bf16[128,7,512]{2,0,1:T(8,128)(2,1)} async-done(((bf16[128,7,512]{2,0,1:T(8,128)(2,1)}), bf16[128,7,512]{2,0,1:T(8,128)(2,1)}) %all-reduce.3.cloned.1.call-update) | async-done | bytes 917520
  443.3 0.8 constant_dynamic-slice_fusion
  444.1 23.2 %all_gather.3 = bf16[4,7,8192]{2,0,1:T(4,128)(2,1)S(1)} all-gather(bf16[4,7,512]{2,0,1:T(4,128)(2,1)S(1)} %constant_dynamic-slice_fusion), channel_id=1, replica_groups=mesh['ctx'=32,'ch'=8,'rep'=2] {'ch','rep'}, dimensions={2}, use_global_device_ids=true | all-gather | bytes 487424 | tf_op jit(solution)/shard_map/all_gather | solution.py:137
  467.4 0.8 copy.106
  (21 shorter events, 0.1 us)
Async XLA Ops:
  7.9 5.7 %collective-permute-start = (bf16[3,2,512]{2,1,0:T(2,128)(2,1)S(1)}, bf16[3,2,512]{2,1,0:T(2,128)(2,1)S(1)}, u32[]{:S(2)}, u32[]{:S(2)}) collective-permute-start(bf16[3,2,512]{2,1,0:T(2,128)(2,1)S(1)} %slice.81), channel_id=1, source_target_pairs={{0,16},{16,32},{32,48},{48,64},{64,80},{80,96},{96,112},{112,128},... | collective-permute-start | bytes 18440 | tf_op jit(solution)/shard_map/ppermute | solution.py:17
  15.0 1.0 copy-start.2
  18.0 37.9 %all-to-all-start = ((f32[2,1,256,512]{3,0,1,2:T(2,128)}), f32[2,1,256,512]{3,0,1,2:T(2,128)S(1)}, u32[]{:S(2)}, u32[]{:S(2)}) async-start(f32[2,1,256,512]{3,0,1,2:T(2,128)} %copy.48), calls=%async_computation | async-start | bytes 2097152 | tf_op jit(solution)/shard_map/all_to_all | solution.py:79
  197.6 8.6 %copy-start.4 = (s32[128]{0:T(128)S(1)}, s32[128]{0:T(128)}, u32[]{:S(2)}) copy-start(s32[128]{0:T(128)} %param.11) | copy-start | bytes 1540
  197.6 8.6 %copy-start = (bf16[3,256,512]{2,1,0:T(8,128)(2,1)S(1)}, bf16[3,256,512]{2,1,0:T(8,128)(2,1)}, u32[]{:S(2)}) copy-start(bf16[3,256,512]{2,1,0:T(8,128)(2,1)} %param.7) | copy-start | bytes 2359300
  197.6 57.8 %all-to-all-start.2 = ((f32[2,2,256,512]{3,1,0,2:T(2,128)}), f32[2,2,256,512]{3,1,0,2:T(2,128)}, u32[]{:S(2)}, u32[]{:S(2)}) async-start(f32[2,2,256,512]{3,1,0,2:T(2,128)} %copy.57), calls=%async_computation.2 | async-start | bytes 4194304 | tf_op jit(solution)/shard_map/all_to_all | solution.py:94
  208.1 1.9 copy-start.5
  208.1 1.9 copy-start.6
  260.9 21.0 %copy-start.3 = (f32[512]{0:T(512)S(1)}, f32[512]{0:T(512)}, u32[]{:S(2)}) copy-start(f32[512]{0:T(512)} %param.9) | copy-start | bytes 6148
  262.1 19.9 %all-to-all-start.3 = ((f32[32,8,512]{2,1,0:T(8,128)}), f32[32,8,512]{2,1,0:T(8,128)S(1)}, u32[]{:S(2)}, u32[]{:S(2)}) async-start(f32[32,8,512]{2,1,0:T(8,128)} %copy.65), calls=%async_computation.3 | async-start | bytes 1048576 | tf_op jit(solution)/shard_map/all_to_all | solution.py:109
  268.2 175.1 %all-reduce.3.cloned.1.call-start = ((), (), s32[]{:S(2)}) async-start(), calls=%async_computation.4 | async-start | bytes 1835008
  282.2 4.1 copy-start.1
Sparse Core Ops, SparseCore 0:
  286.5 156.7 all-reduce.2
where the time goes:
time: 484 us; the launch traced here: 475 us
  waiting for transfers between devices  234 us (48%)
  blocking collectives  123 us (25%)
  matrix products  37 us (8%)
  starting transfers between devices  33 us (7%)
  local copies, waits for them, and re-layouts  27.3 us (6%)
  between operations  15.3 us (3%)
  other arithmetic  5.17 us (1%)
    unnamed x2, waiting for transfers between devices  155 us
    all_to_all x1, blocking collectives, body(): lax.all_to_all(forward_local(spread, my_index), 'ctx', split_axis=2, conc...  99.9 us
    all_to_all x1, waiting for transfers between devices, body(): lax.all_to_all(jnp.stack([back_re, back_im]), 'ctx', split_axis=2, concat...  44.1 us
    all_to_all x1, waiting for transfers between devices, body(): lax.all_to_all(stacked, 'ctx', split_axis=2, concat_axis=1, tiled=True)  24.3 us
    all_gather x1, blocking collectives, body(): states = lax.all_gather(my_states, ('ch', 'rep'), axis=2, tiled=True)  23.2 us
    all_to_all x1, starting transfers between devices, body(): lax.all_to_all(stacked, 'ctx', split_axis=2, concat_axis=1, tiled=True)  13.5 us
    all_to_all x1, waiting for transfers between devices, body(): lax.all_to_all(block_vals, 'ctx', split_axis=0, concat_axis=1, tiled=True)  11 us
  transfers between devices with their start and end apart: 5, of which 4 were waited for; matrix products, arithmetic and copies ran while one was open for 2% of the time, Pallas kernels for 0%

commit v1 on v0

v1 whole, which is shorter than its diff:
```python
import math

import jax
import jax.numpy as jnp
import ml_dtypes
import numpy as np
from jax import lax
from jax.experimental import pallas as pl
from jax.experimental.pallas import tpu as pltpu
from jax.sharding import PartitionSpec as P

MESH = pl.DeviceIdType.MESH
F32 = jnp.float32
BF16 = jnp.bfloat16

N_CTX = 32
CH = 16
TOK = 256
SEQ = 8192
LEN_A = 64
LEN_B = 128
SLOTS = 4


def split_np(table):
    high = table.astype(ml_dtypes.bfloat16)
    low = (table - high.astype(np.float64)).astype(ml_dtypes.bfloat16)
    return high, low


def tables():
    k = np.arange(LEN_A) + 0.25
    theta = 2.0 * np.pi * np.outer(k, np.arange(LEN_A)) / LEN_A
    outer = np.concatenate([np.cos(theta), -np.sin(theta)], axis=0)
    o_high, o_low = split_np(outer)
    first = np.concatenate([o_high, o_high, o_low], axis=1)
    e_high, e_low = split_np(outer.T / SEQ)
    last = np.concatenate([e_high, e_low], axis=1)
    phi = 2.0 * np.pi * np.outer(np.arange(LEN_B), np.arange(LEN_B)) / LEN_B
    c, s = np.cos(phi), np.sin(phi)
    inner = np.block([[c, -s], [s, c]])
    i_high, i_low = split_np(inner)
    v_high, v_low = split_np(inner.T)
    inner_all = np.stack([i_high, i_low, v_high, v_low])
    turn = 2.0 * np.pi * np.outer(k, np.arange(LEN_B)) / SEQ
    turns = np.stack([np.tile(np.cos(turn), (1, 2)), np.tile(np.sin(turn), (1, 2))]).astype(np.float32)
    row, col = np.arange(256)[:, None], np.arange(512)[None, :]
    place = np.stack(
        [(row % 128 == col // 4) & (row // 128 + 2 * p == col % 4) for p in (0, 1)]
    ).astype(ml_dtypes.bfloat16)
    return first, last, inner_all, turns, place


def split(value):
    high = value.astype(BF16)
    return high, (value - high.astype(F32)).astype(BF16)


def dot(a, b):
    return jnp.dot(a, b, preferred_element_type=F32)


def kernel(
    proj_hbm, filt_hbm, taps_ref, gain_ref, ends_ref, repl_ref, slot_ref,
    first_ref, last_ref, inner_ref, turns_ref, place_ref,
    out_ref, states_ref,
    proj, filt, f_send, kv_send, q_send, o_send, e_send, l_send,
    f_recv, kv_recv, q_recv, o_recv, e_recv, l_recv, ge_recv, gl_recv,
    spec, sig, mixed, onehot, taps_t, tmp,
    local_sem, send_sem, recv_sem,
):
    me = lax.axis_index("ctx")
    ch, rep = lax.axis_index("ch"), lax.axis_index("rep")
    mine = ch * 2 + rep

    load_f = pltpu.make_async_copy(filt_hbm, filt, local_sem.at[0])
    load_p = pltpu.make_async_copy(proj_hbm, proj, local_sem.at[1])
    load_f.start()
    load_p.start()

    barrier = pltpu.get_barrier_semaphore()

    def greet_ctx(t, carry):
        pl.semaphore_signal(
            barrier, inc=1, device_id={"ctx": lax.rem(me + t, N_CTX)}, device_id_type=MESH
        )
        return carry

    def near(t):
        other = lax.rem(mine + t, 16)
        return {"ch": other // 2, "rep": lax.rem(other, 2)}

    def greet_near(t, carry):
        pl.semaphore_signal(barrier, inc=1, device_id=near(t), device_id_type=MESH)
        return carry

    lax.fori_loop(1, N_CTX, greet_ctx, 0)
    lax.fori_loop(1, 16, greet_near, 0)

    def send_ctx(n, source, target):
        def one(t, carry):
            peer = lax.rem(me + t, N_CTX)
            pltpu.make_async_remote_copy(
                src_ref=source(peer), dst_ref=target.at[me],
                send_sem=send_sem.at[n], recv_sem=recv_sem.at[n],
                device_id={"ctx": peer}, device_id_type=MESH,
            ).start()
            return carry

        lax.fori_loop(1, N_CTX, one, 0)

    def send_near(n, buffer):
        def one(t, carry):
            pltpu.make_async_remote_copy(
                src_ref=buffer.at[mine], dst_ref=buffer.at[mine],
                send_sem=send_sem.at[n], recv_sem=recv_sem.at[n],
                device_id=near(t), device_id_type=MESH,
            ).start()
            return carry

        lax.fori_loop(1, 16, one, 0)

    def await_bytes(buffer, count, sem):
        part = buffer.at[pl.ds(0, count)]
        pltpu.make_async_copy(part, part, sem).wait()

    load_f.wait()
    for g in range(4):
        block = filt[:, 128 * g : 128 * g + 128].T
        for h in range(2):
            f_send[8 * g : 8 * g + 8, CH * h : CH * h + CH] = (
                block[:, 128 * h : 128 * h + 128].reshape(8, CH, 128)
            )
    pl.semaphore_wait(barrier, N_CTX - 1 + 15)
    send_ctx(0, lambda peer: f_send.at[peer], f_recv)
    f_recv[me] = f_send[me]

    load_p.wait()
    for p in (1, 2):
        for g in range(4):
            kv_send[8 * g : 8 * g + 8, 16 * (p - 1) : 16 * p] = (
                proj[p, :, 128 * g : 128 * g + 128].T.reshape(8, CH, TOK)
            )
    send_ctx(1, lambda peer: kv_send.at[peer], kv_recv)
    kv_recv[me] = kv_send[me]
    for g in range(4):
        q_send[8 * g : 8 * g + 8] = proj[0, :, 128 * g : 128 * g + 128].T.reshape(8, CH, TOK)
    send_ctx(2, lambda peer: q_send.at[peer], q_recv)
    q_recv[me] = q_send[me]

    rows = [taps_ref[p] for p in range(3)] + [gain_ref[...], jnp.zeros((6, 512), F32)]
    taps_t[...] = jnp.concatenate(rows, axis=0).T
    my_taps = taps_t[pl.ds(pl.multiple_of(me * CH, CH), CH), :]

    def column(n):
        return jnp.broadcast_to(my_taps[:, n : n + 1], (CH, TOK))

    target = repl_ref[...] * SLOTS + slot_ref[...]
    target_rows = jnp.broadcast_to(target, (128, 128)).T
    ends_rows = jnp.broadcast_to(ends_ref[...], (128, 128)).T
    slots_here = lax.broadcasted_iota(jnp.int32, (128, 128), 1)
    by_slot = jnp.sum(jnp.where(target_rows == slots_here, ends_rows, 0), axis=0, keepdims=True)
    wanted = jnp.concatenate([by_slot - 1, by_slot], axis=1)
    token = lax.broadcasted_iota(jnp.int32, (TOK, 256), 0)

    def pick(i, carry):
        onehot[i] = jnp.where(token + i * TOK == wanted, 1.0, 0.0).astype(BF16)
        return carry

    lax.fori_loop(0, N_CTX, pick, 0)

    cos_t, sin_t = turns_ref[0], turns_ref[1]

    def forward(ref, c):
        x = jnp.concatenate(
            [ref[pl.ds(c + n, LEN_A, stride=CH), :] for n in range(2)], axis=1
        )
        high, low = split(x)
        z = dot(first_ref[...], jnp.concatenate([high, low, high], axis=0))
        re, im = z[:64], z[64:]
        zr = re * cos_t + im * sin_t
        zi = im * cos_t - re * sin_t
        z = jnp.concatenate(
            [
                jnp.concatenate([zr[:, :128], zi[:, :128]], axis=1),
                jnp.concatenate([zr[:, 128:], zi[:, 128:]], axis=1),
            ],
            axis=0,
        )
        high, low = split(z)
        return dot(high, inner_ref[0]) + (dot(low, inner_ref[0]) + dot(high, inner_ref[1]))

    await_bytes(f_recv, N_CTX - 1, recv_sem.at[0])
    flat_f = f_recv.reshape(LEN_A * CH, 128)

    def filter_pair(m, carry):
        spec[pl.ds(pl.multiple_of(128 * m, 128), 128), :] = forward(flat_f, 2 * m)
        return carry

    lax.fori_loop(0, CH // 2, filter_pair, 0)

    lane = lax.broadcasted_iota(jnp.int32, (2 * CH, TOK), 1)
    kv_taps = [jnp.concatenate([column(3 + j), column(6 + j)], axis=0) for j in range(3)]
    await_bytes(kv_recv, N_CTX - 1, recv_sem.at[1])

    def signal_block(i, carry):
        before1, before2 = carry
        x = kv_recv[i].astype(F32)
        roll1, roll2 = pltpu.roll(x, 1, 1), pltpu.roll(x, 2, 1)
        conv = (
            kv_taps[0] * x
            + kv_taps[1] * jnp.where(lane < 1, before1, roll1)
            + kv_taps[2] * jnp.where(lane < 2, before2, roll2)
        )
        signal = conv[:CH] * conv[CH:]
        sig[pl.ds(pl.multiple_of(i * 2 * CH, 2 * CH), 2 * CH), :] = jnp.concatenate(
            [signal[:, :128], signal[:, 128:]], axis=0
        )
        return roll1, roll2

    zero = jnp.zeros((2 * CH, TOK), F32)
    lax.fori_loop(0, N_CTX, signal_block, (zero, zero))

    def gather_kv(i, total):
        return total + dot(kv_recv[i], onehot[i])

    rows_kv = lax.fori_loop(0, N_CTX, gather_kv, jnp.zeros((2 * CH, 256), F32)).astype(BF16)
    early = dot(rows_kv[:CH], place_ref[0]) + dot(rows_kv[CH:], place_ref[1])
    for g in range(4):
        e_send[g] = early[:, 128 * g : 128 * g + 128].astype(BF16)
    send_ctx(3, lambda peer: e_send.at[peer // 8], e_recv)
    e_recv[me] = e_send[me // 8]

    def convolve_pair(m, carry):
        x = forward(sig, 2 * m)
        f = spec[pl.ds(pl.multiple_of(128 * m, 128), 128), :]
        xr, xi, fr, fi = x[:, :128], x[:, 128:], f[:, :128], f[:, 128:]
        y = jnp.concatenate([xr * fr - xi * fi, xr * fi + xi * fr], axis=1)
        high, low = split(y)
        u = dot(high, inner_ref[2]) + (dot(low, inner_ref[2]) + dot(high, inner_ref[3]))
        ur = jnp.concatenate([u[:64, :128], u[64:, :128]], axis=1)
        ui = jnp.concatenate([u[:64, 128:], u[64:, 128:]], axis=1)
        w = jnp.concatenate([ur * cos_t - ui * sin_t, ui * cos_t + ur * sin_t], axis=0)
        high, low = split(w)
        y = dot(last_ref[...], jnp.concatenate([high, high], axis=0)) + dot(last_ref[:, :128], low)
        mixed[pl.ds(2 * m, LEN_A, stride=CH), :] = y[:, :128]
        mixed[pl.ds(2 * m + 1, LEN_A, stride=CH), :] = y[:, 128:]
        return carry

    lax.fori_loop(0, CH // 2, convolve_pair, 0)

    q_taps = [column(j) for j in range(3)]
    gain = column(9)
    lane_q = lax.broadcasted_iota(jnp.int32, (CH, TOK), 1)
    await_bytes(q_recv, N_CTX - 1, recv_sem.at[2])

    def gate_block(i, carry):
        before1, before2 = carry
        x = q_recv[i].astype(F32)
        roll1, roll2 = pltpu.roll(x, 1, 1), pltpu.roll(x, 2, 1)
        conv = (
            q_taps[0] * x
            + q_taps[1] * jnp.where(lane_q < 1, before1, roll1)
            + q_taps[2] * jnp.where(lane_q < 2, before2, roll2)
        )
        for h in range(2):
            here = pl.ds(pl.multiple_of((2 * i + h) * CH, CH), CH)
            half = slice(128 * h, 128 * h + 128)
            o_send[i, :, half] = (
                conv[:, half] * (mixed[here, :] + gain[:, half] * sig[here, :])
            ).astype(BF16)
        return roll1, roll2

    zero_q = jnp.zeros((CH, TOK), F32)
    lax.fori_loop(0, N_CTX, gate_block, (zero_q, zero_q))

    def gather_q(i, total):
        both = jnp.concatenate([q_recv[i], o_send[i]], axis=0)
        return total + dot(both, onehot[i])

    rows_q = lax.fori_loop(0, N_CTX, gather_q, jnp.zeros((2 * CH, 256), F32)).astype(BF16)
    late = dot(rows_q[:CH], place_ref[0]) + dot(rows_q[CH:, 128:], place_ref[1, :128])
    for g in range(4):
        l_send[g] = late[:, 128 * g : 128 * g + 128].astype(BF16)
    send_ctx(4, lambda peer: l_send.at[peer // 8], l_recv)
    send_ctx(5, lambda peer: o_send.at[peer], o_recv)
    l_recv[me] = l_send[me // 8]
    o_recv[me] = o_send[me]

    mine_rows = pl.ds(pl.multiple_of(lax.rem(me, 8) * 16, 16), 16)

    def own_rows(received):
        tmp[...] = received[...].reshape(N_CTX * CH, 128).astype(F32).T
        return tmp[mine_rows, :].astype(BF16)

    await_bytes(e_recv, N_CTX - 1, recv_sem.at[3])
    ge_recv[mine] = own_rows(e_recv)
    send_near(6, ge_recv)
    await_bytes(l_recv, N_CTX - 1, recv_sem.at[4])
    gl_recv[mine] = own_rows(l_recv)
    send_near(7, gl_recv)

    await_bytes(o_recv, N_CTX - 1, recv_sem.at[5])
    for g in range(4):
        out_ref[:, 128 * g : 128 * g + 128] = o_recv[8 * g : 8 * g + 8].reshape(128, TOK).T

    await_bytes(ge_recv, 15, recv_sem.at[6])
    await_bytes(gl_recv, 15, recv_sem.at[7])
    for j in range(16):
        kv, qo = ge_recv[j].astype(F32), gl_recv[j].astype(F32)
        for s in range(SLOTS):
            r = 4 * s
            block = jnp.concatenate([qo[r : r + 2], kv[r : r + 4], qo[r + 2 : r + 3]], axis=0)
            states_ref[s, :, 512 * j : 512 * j + 512] = block.astype(BF16)

    await_bytes(f_send, N_CTX - 1, send_sem.at[0])
    await_bytes(kv_send, N_CTX - 1, send_sem.at[1])
    await_bytes(q_send, N_CTX - 1, send_sem.at[2])
    await_bytes(e_recv, N_CTX - 1, send_sem.at[3])
    await_bytes(l_recv, N_CTX - 1, send_sem.at[4])
    await_bytes(o_send, N_CTX - 1, send_sem.at[5])
    await_bytes(ge_recv, 15, send_sem.at[6])
    await_bytes(gl_recv, 15, send_sem.at[7])


def body(projections, short_taps, skip_gain, long_filter, request_ends, replica_of, slot_index):
    first, last, inner, turns, place = tables()
    whole = pl.BlockSpec(memory_space=pltpu.VMEM)
    hbm = pl.BlockSpec(memory_space=pl.ANY)

    def blocks(rows, lanes, dtype, count=N_CTX):
        return pltpu.VMEM((count, rows, lanes), dtype)

    return pl.pallas_call(
        kernel,
        out_shape=(
            jax.ShapeDtypeStruct((TOK, 512), BF16),
            jax.ShapeDtypeStruct((SLOTS, 7, 8192), BF16),
        ),
        in_specs=[hbm, hbm] + [whole] * 10,
        out_specs=(whole, whole),
        scratch_shapes=[
            pltpu.VMEM((3, TOK, 512), BF16),
            pltpu.VMEM((TOK, 512), F32),
            blocks(2 * CH, 128, F32), blocks(2 * CH, TOK, BF16), blocks(CH, TOK, BF16), blocks(CH, TOK, BF16),
            blocks(CH, 128, BF16, 4), blocks(CH, 128, BF16, 4),
            blocks(2 * CH, 128, F32), blocks(2 * CH, TOK, BF16), blocks(CH, TOK, BF16), blocks(CH, TOK, BF16),
            blocks(CH, 128, BF16), blocks(CH, 128, BF16),
            blocks(16, 512, BF16, 16), blocks(16, 512, BF16, 16),
            pltpu.VMEM((64 * CH, 256), F32),
            pltpu.VMEM((LEN_A * CH, 128), F32),
            pltpu.VMEM((LEN_A * CH, 128), F32),
            blocks(TOK, 256, BF16),
            pltpu.VMEM((512, 16), F32),
            pltpu.VMEM((128, 512), F32),
            pltpu.SemaphoreType.DMA((2,)),
            pltpu.SemaphoreType.DMA((8,)),
            pltpu.SemaphoreType.DMA((8,)),
        ],
        compiler_params=pltpu.CompilerParams(
            collective_id=0, has_side_effects=True, vmem_limit_bytes=48 * 2**20
        ),
        cost_estimate=pl.CostEstimate(flops=2 * 10**9, bytes_accessed=4 * 10**6, transcendentals=0),
    )(
        projections, long_filter, short_taps, skip_gain.reshape(1, 512),
        request_ends.reshape(1, 128), replica_of.reshape(1, 128), slot_index.reshape(1, 128),
        jnp.asarray(first), jnp.asarray(last), jnp.asarray(inner), jnp.asarray(turns), jnp.asarray(place),
    )


def solution(mesh):
    return jax.shard_map(
        body,
        mesh=mesh,
        in_specs=(
            P(None, "ctx", ("ch", "rep")),
            P(None, None, ("ch", "rep")),
            P(("ch", "rep")),
            P("ctx", ("ch", "rep")),
            P(),
            P(),
            P(),
        ),
        out_specs=(P("ctx", ("ch", "rep")), P("ctx", None, None)),
        check_vma=False,
    )
```

time: 484 us -> 91.3 us (0.19); the launches traced: 475 us -> 90.8 us
  waiting for transfers between devices: 234 us -> 0 us
  blocking collectives: 123 us -> 0 us
  Pallas kernels: 0 us -> 80.1 us
  matrix products: 37 us -> 0 us
  starting transfers between devices: 33 us -> 0 us
  local copies, waits for them, and re-layouts: 27.3 us -> 10 us
  between operations: 15.3 us -> 0.68 us
  other arithmetic: 5.17 us -> 0 us
    unnamed x2 -> x0, waiting for transfers between devices: 155 us -> none
    all_to_all x1 -> x0, blocking collectives: 99.9 us -> none  [body(): lax.all_to_all(forward_local(spread, my_index), 'ctx', split_axis=2, conc...]
    pallas_call x0 -> x1, Pallas kernels: none -> 80.1 us  [body(): pl.pallas_call(kernel, out_shape=(jax.ShapeDtypeStruct((TOK, 512), BF16),...]
    all_to_all x3 -> x0, waiting for transfers between devices: 79.3 us -> none  [the longest x1 44.1 us: body(): lax.all_to_all(jnp.stack([back_re, back_im]), 'ctx', split_axis=2, concat...]
    dot_general x13 -> x0, matrix products: 37 us -> none  [the longest x1 4.88 us: forward_finish(): jnp.einsum('kb,smbc->smkc', sin_b, turned_im, precision=highest)]
    all_to_all x3 -> x0, starting transfers between devices: 28.1 us -> none  [the longest x1 13.5 us: body(): lax.all_to_all(stacked, 'ctx', split_axis=2, concat_axis=1, tiled=True)]
    all_gather x1 -> x0, blocking collectives: 23.2 us -> none  [body(): states = lax.all_gather(my_states, ('ch', 'rep'), axis=2, tiled=True)]
    another operation x3 -> x0, local copies, waits for them, and re-layouts: 7.25 us -> none  [the longest x1 4.15 us: body(): jnp.stack([back_re, back_im])]
  transfers between devices with their start and end apart: 5 -> 0, of which waited for: 4 -> 0; matrix products, arithmetic and copies ran while one was open for 2% -> 0% of each run, Pallas kernels for 0% -> 0%
where the time goes in v1:
time: 91.3 us; the launch traced here: 90.8 us
  Pallas kernels  80.1 us (88%)
  local copies, waits for them, and re-layouts  10 us (11%)
    pallas_call x1, Pallas kernels, body(): pl.pallas_call(kernel, out_shape=(jax.ShapeDtypeStruct((TOK, 512), BF16),...  80.1 us
    unnamed x25, local copies, waits for them, and re-layouts  8.87 us

profile of v1, /device:TPU:1, one launch (start us, length us, event | category | flops | bytes accessed | tf_op | source)
XLA Modules:
  0.0 90.8 jit_solution(6187252764712707051)
XLA Ops:
  0.6 0.0 copy-start.3
  0.6 0.0 copy-start.4
  0.7 0.0 copy-start.5
  0.7 0.0 copy-start.6
  0.7 0.6 copy-done.3
  1.3 0.0 copy-done.4
  1.3 0.0 copy-done.5
  1.3 0.0 copy-done.6
  1.3 0.0 copy-start
  1.3 1.1 %copy-done = bf16[3,256,512]{2,1,0:T(8,128)(2,1)S(1)} copy-done((bf16[3,256,512]{2,1,0:T(8,128)(2,1)S(1)}, bf16[3,256,512]{2,1,0:T(8,128)(2,1)}, u32[]{:S(2)}) %copy-start) | copy-done | bytes 786456
  2.5 0.0 copy-start.1
  2.5 1.0 %copy-done.1 = f32[256,512]{1,0:T(8,128)S(1)} copy-done((f32[256,512]{1,0:T(8,128)S(1)}, f32[256,512]{1,0:T(8,128)}, u32[]{:S(2)}) %copy-start.1) | copy-done | bytes 524312
  3.5 0.0 copy-start.2
  3.5 0.7 copy-done.2
  4.2 0.0 copy-start.7
  4.3 1.0 %copy-done.7 = bf16[2,256,512]{2,1,0:T(8,128)(2,1)S(1)} copy-done((bf16[2,256,512]{2,1,0:T(8,128)(2,1)S(1)}, bf16[2,256,512]{2,1,0:T(8,128)(2,1)}, u32[]{:S(2)}) %copy-start.7) | copy-done | bytes 524312
  5.3 0.0 copy-start.8
  5.3 1.0 %copy-done.8 = bf16[4,256,256]{2,1,0:T(8,128)(2,1)S(1)} copy-done((bf16[4,256,256]{2,1,0:T(8,128)(2,1)S(1)}, bf16[4,256,256]{2,1,0:T(8,128)(2,1)}, u32[]{:S(2)}) %copy-start.8) | copy-done | bytes 524312
  6.3 0.0 copy-start.9
  6.3 0.9 copy-done.9
  7.2 0.0 copy-start.10
  7.2 0.8 copy-done.10
  8.1 0.0 copy-start.11
  8.1 0.8 copy-done.11
  8.8 80.1 %shard_map.131 = (bf16[256,512]{1,0:T(8,128)(2,1)S(1)}, bf16[4,7,8192]{2,1,0:T(8,128)(2,1)S(1)}) custom-call(bf16[3,256,512]{2,1,0:T(8,128)(2,1)S(1)} %copy-done, f32[256,512]{1,0:T(8,128)S(1)} %copy-done.1, f32[3,3,512]{2,1,0:T(4,128)S(1)} %copy-done.2, f32[1,512]{1,0:T(1,128)S(1)} %bitcast.4, s32[1,128]{1,0:T(1,128)S(1)} %bitcast.5, s32[1,128]{1,0:T(1,128)S(1)} %bitcast.6, ...), custom_call_target="tpu_custom_call" | custom-call | flops 2000000000 | bytes 4000000 | tf_op jit(solution)/shard_map/pallas_call | solution.py:334
  88.9 1.2 %copy.14 = bf16[4,7,8192]{2,0,1:T(4,128)(2,1)} copy(bf16[4,7,8192]{2,1,0:T(8,128)(2,1)S(1)} %get-tuple-element.3) | data formatting | bytes 917504 | tf_op jit(solution)/shard_map/pallas_call | solution.py:334
  90.1 0.7 copy.16
Async XLA Ops:
  0.6 0.7 copy-start.3
  0.6 0.7 copy-start.4
  0.7 0.7 copy-start.5
  0.7 0.7 copy-start.6
  1.3 1.1 %copy-start = (bf16[3,256,512]{2,1,0:T(8,128)(2,1)S(1)}, bf16[3,256,512]{2,1,0:T(8,128)(2,1)}, u32[]{:S(2)}) copy-start(bf16[3,256,512]{2,1,0:T(8,128)(2,1)} %proj_hbm.1) | copy-start | bytes 2359300
  2.5 1.0 %copy-start.1 = (f32[256,512]{1,0:T(8,128)S(1)}, f32[256,512]{1,0:T(8,128)}, u32[]{:S(2)}) copy-start(f32[256,512]{1,0:T(8,128)} %filt_hbm.1) | copy-start | bytes 1572868
  3.5 0.7 copy-start.2
  4.2 1.0 %copy-start.7 = (bf16[2,256,512]{2,1,0:T(8,128)(2,1)S(1)}, bf16[2,256,512]{2,1,0:T(8,128)(2,1)}, u32[]{:S(2)}) copy-start(bf16[2,256,512]{2,1,0:T(8,128)(2,1)} %constant.14.clone.place_ref) | copy-start | bytes 1572868
  5.3 1.0 %copy-start.8 = (bf16[4,256,256]{2,1,0:T(8,128)(2,1)S(1)}, bf16[4,256,256]{2,1,0:T(8,128)(2,1)}, u32[]{:S(2)}) copy-start(bf16[4,256,256]{2,1,0:T(8,128)(2,1)} %constant.12.clone.inner_ref) | copy-start | bytes 1572868
  6.3 0.9 copy-start.9
  7.2 0.8 copy-start.10
  8.1 0.8 copy-start.11

commit v2 on v1

v2 whole, which is shorter than its diff:
```python
import math

import jax
import jax.numpy as jnp
import ml_dtypes
import numpy as np
from jax import lax
from jax.experimental import pallas as pl
from jax.experimental.pallas import tpu as pltpu
from jax.sharding import PartitionSpec as P

MESH = pl.DeviceIdType.MESH
F32 = jnp.float32
BF16 = jnp.bfloat16

N_CTX = 32
CH = 16
TOK = 256
SEQ = 8192
LEN_A = 64
LEN_B = 128
SLOTS = 4
TOP = 32767.0


def split_np(table):
    high = table.astype(ml_dtypes.bfloat16)
    low = (table - high.astype(np.float64)).astype(ml_dtypes.bfloat16)
    return high, low


def tables():
    k = np.arange(LEN_A) + 0.25
    theta = 2.0 * np.pi * np.outer(k, np.arange(LEN_A)) / LEN_A
    outer = np.concatenate([np.cos(theta), -np.sin(theta)], axis=0)
    o_high, o_low = split_np(outer)
    first = np.concatenate([o_high, o_high, o_low], axis=1)
    e_high, e_low = split_np(outer.T / SEQ)
    last = np.concatenate([e_high, e_low], axis=1)
    phi = 2.0 * np.pi * np.outer(np.arange(LEN_B), np.arange(LEN_B)) / LEN_B
    c, s = np.cos(phi), np.sin(phi)
    inner = np.block([[c, -s], [s, c]])
    i_high, i_low = split_np(inner)
    v_high, v_low = split_np(inner.T)
    inner_all = np.stack([i_high, i_low, v_high, v_low])
    turn = 2.0 * np.pi * np.outer(k, np.arange(LEN_B)) / SEQ
    turns = np.stack([np.tile(np.cos(turn), (1, 2)), np.tile(np.sin(turn), (1, 2))]).astype(np.float32)
    return first, last, inner_all, turns


def row_scale(block, axis):
    largest = jnp.max(jnp.abs(block), axis=axis, keepdims=True)
    step = jnp.maximum(largest, 2.0**-100) * (1.0078125 / TOP)
    return step.astype(BF16).astype(F32)


def code(scaled):
    return jnp.floor(scaled + 0.5).astype(jnp.int32).astype(jnp.int16)


def decode(codes):
    return codes.astype(jnp.int32).astype(F32)


def iota(shape, axis):
    return lax.broadcasted_iota(jnp.int32, shape, axis)


def split(value):
    high = value.astype(BF16)
    return high, (value - high.astype(F32)).astype(BF16)


def dot(a, b):
    return jnp.dot(a, b, preferred_element_type=F32)


def kernel(*refs):
    hbm_refs, (out_ref, states_ref), vmem_refs = refs[:11], refs[11:13], refs[13:24]
    (
        proj, filt, taps_ref, gain_ref, ends_ref, repl_ref, slot_ref,
        first_ref, last_ref, inner_ref, turns_ref,
    ) = vmem_refs
    (
        halo_send, halo_recv, f_send, s_send, m_send, r_send, e_send, l_send,
        f_recv, s_recv, m_recv, r_recv, e_recv, l_recv, ge_recv, gl_recv,
        spec, filter_t, sig_t, mixed, query, signal, steps, onehot, taps_t, tmp,
        local_sem, send_sem, recv_sem,
    ) = refs[24:]
    me = lax.axis_index("ctx")
    ch, rep = lax.axis_index("ch"), lax.axis_index("rep")
    my_x, my_z = me // 8, lax.rem(me, 8)
    after = {"ctx": lax.rem(me + 1, N_CTX)}
    sibling = {"rep": 1 - rep}

    loads = [
        pltpu.make_async_copy(source, target, local_sem.at[n])
        for n, (source, target) in enumerate(zip(hbm_refs, vmem_refs))
    ]
    for load in loads:
        load.start()

    barrier = pltpu.get_barrier_semaphore()

    def greet(device):
        pl.semaphore_signal(barrier, inc=1, device_id=device, device_id_type=MESH)

    def greet_ctx(t, carry):
        greet({"ctx": lax.rem(me + t, N_CTX)})
        return carry

    def greet_ch(t, carry):
        greet({"ch": lax.rem(ch + t, 8)})
        return carry

    lax.fori_loop(1, N_CTX, greet_ctx, 0)
    lax.fori_loop(1, 8, greet_ch, 0)
    greet(sibling)

    def remote(n, source, target, device):
        return pltpu.make_async_remote_copy(
            src_ref=source, dst_ref=target,
            send_sem=send_sem.at[n], recv_sem=recv_sem.at[n],
            device_id=device, device_id_type=MESH,
        )

    def send_line(n, source, target, dx):
        x = lax.rem(my_x + dx, 4)

        def one(t, carry):
            peer = 8 * x + lax.rem(my_z + t, 8)
            remote(n, source(peer), target.at[me], {"ctx": peer}).start()
            return carry

        lax.fori_loop(1 if dx == 0 else 0, 8, one, 0)

    def send_ctx(n, source, target):
        for dx in range(4):
            send_line(n, source, target, dx)

    def send_ch(n, buffer):
        def one(t, carry):
            remote(n, buffer.at[rep, ch], buffer.at[rep, ch], {"ch": lax.rem(ch + t, 8)}).start()
            return carry

        lax.fori_loop(1, 8, one, 0)

    def await_bytes(part, sem):
        pltpu.make_async_copy(part, part, sem).wait()

    def others(buffer):
        return buffer.at[pl.ds(0, N_CTX - 1)]

    def seven(buffer):
        return buffer.at[0, pl.ds(0, 7)]

    def column_block(dx):
        g = lax.rem(my_x + dx, 4)
        return pl.ds(pl.multiple_of(8 * g, 8), 8), pl.ds(pl.multiple_of(128 * g, 128), 128)

    def put_codes(block, kind, dx, target):
        devices, lanes = column_block(dx)
        step = row_scale(block, 0)
        steps[kind : kind + 1, lanes] = step
        turned = (block * (1.0 / step)).T
        for h in range(2):
            target[devices, CH * h : CH * h + CH] = code(
                turned[:, 128 * h : 128 * h + 128]
            ).reshape(8, CH, 128)

    def put_filter(dx):
        put_codes(filt[:, column_block(dx)[1]], 0, dx, f_send)

    loads[0].wait()
    halo_send[...] = jnp.concatenate(
        [proj[p, TOK - 16 :, :].astype(F32)[14:] for p in range(3)] + [jnp.zeros((2, 512), F32)], axis=0
    )
    steps[...] = jnp.zeros((8, 512), F32)
    loads[1].wait()
    put_filter(0)
    pl.semaphore_wait(barrier, N_CTX - 1 + 7 + 1)
    halo_copy = remote(0, halo_send, halo_recv, after)
    halo_copy.start()
    for dx in range(4):
        if dx > 0:
            put_filter(dx)
        send_line(1, lambda peer: f_send.at[peer], f_recv, dx)
    f_recv[me] = f_send[me]
    for load in loads[2:]:
        load.wait()

    ends = ends_ref[...]
    end_block = ends // TOK
    end_lane = ends - end_block * TOK

    def down(row):
        return jnp.broadcast_to(row, (128, 128)).T

    earlier = iota((128, 128), 0) < iota((128, 128), 1)
    same = down(end_block) == end_block
    rank = jnp.sum(jnp.where(earlier, jnp.where(same, 1, 0), 0), axis=0, keepdims=True)
    slot_of = down(repl_ref[...] * SLOTS + slot_ref[...])

    def at_slot(row, slots):
        values = down(row)[:, :1]
        hit = slot_of[:, :1] == slots
        return jnp.sum(jnp.where(hit, values, 0), axis=0, keepdims=True)

    where_code = end_block * 16 + rank
    column = iota((128, 1024), 1)
    e_code = at_slot(where_code, column // 32 * 4 + column % 4)
    slots_row = iota((128, 128), 1)
    t_code = at_slot(where_code, slots_row)
    t_end = at_slot(ends, slots_row)
    row_kind = iota((1, 1024), 1) % 32 // 4
    code_all = jnp.concatenate([e_code, t_code, t_code, t_code], axis=1)
    kind_all = jnp.concatenate(
        [jnp.where(row_kind < 6, row_kind + 1, -10)] + [jnp.full((1, 128), k, jnp.int32) for k in range(3)],
        axis=1,
    )
    block_all = code_all // 16
    lane_all = kind_all * 16 + (code_all - block_all * 16)
    onehot[...] = jnp.where(iota((128, 1408), 0) == lane_all, 1.0, 0.0).astype(BF16)

    mine = jnp.where(end_block == me, jnp.where(rank == iota((16, 128), 0), end_lane + 100, 0), 0)
    place = jnp.sum(mine, axis=1, keepdims=True) - 100
    token = iota((16, TOK), 1)

    def rows_at(back):
        return jnp.where(token == place - back, 1.0, 0.0).astype(BF16)

    two_rows = jnp.concatenate([rows_at(1), rows_at(0)], axis=0)
    three_rows = jnp.concatenate([rows_at(2), two_rows], axis=0)

    halo_copy.wait_recv()
    token_row = iota((TOK, 128), 0)
    for dx in range(4):
        devices, lanes = column_block(dx)
        conv = []
        halo_here = jnp.where(me > 0, halo_recv[:, lanes], 0.0)
        for p in range(3):
            x = proj[p, :, lanes].astype(F32)
            tail2, tail1 = halo_here[2 * p : 2 * p + 1], halo_here[2 * p + 1 : 2 * p + 2]
            back1 = jnp.where(token_row < 1, tail1, pltpu.roll(x, 1, 0))
            back2 = jnp.where(
                token_row < 1, tail2, jnp.where(token_row < 2, tail1, pltpu.roll(x, 2, 0))
            )
            taps = taps_ref[p, :, lanes]
            conv.append(taps[0:1] * x + taps[1:2] * back1 + taps[2:3] * back2)
        query[:, lanes] = conv[0]
        product = conv[1] * conv[2]
        signal[:, lanes] = product
        put_codes(product, 1, dx, s_send)
        q_rows = dot(three_rows, proj[0, :, lanes])
        first_rows = q_rows[:16] + jnp.where(place == 1, halo_here[1:2], 0.0)
        rows = jnp.concatenate(
            [
                first_rows, q_rows[16:], dot(two_rows, proj[1, :, lanes]), dot(two_rows, proj[2, :, lanes]),
                steps[:, lanes], jnp.zeros((8, 128), F32),
            ],
            axis=0,
        )
        r_send[devices] = rows.T.astype(BF16).reshape(8, CH, 128)
        send_line(2, lambda peer: r_send.at[peer], r_recv, dx)
    r_recv[me] = r_send[me]
    send_ctx(3, lambda peer: s_send.at[peer], s_recv)
    s_recv[me] = s_send[me]

    rows = [taps_ref[p] for p in range(3)] + [gain_ref[...], jnp.zeros((6, 512), F32)]
    taps_t[...] = jnp.concatenate(rows, axis=0).T
    my_taps = taps_t[pl.ds(pl.multiple_of(me * CH, CH), CH), :]

    cos_t, sin_t = turns_ref[0], turns_ref[1]

    def read_codes(received, target, lane):
        def one(i, carry):
            step = r_recv[i].astype(F32)[:, lane : lane + 1]
            step = jnp.concatenate([step, step], axis=0)
            target[pl.ds(pl.multiple_of(i * 32, 32), 32), :] = decode(received[i]) * step
            return carry

        lax.fori_loop(0, N_CTX, one, 0, unroll=4)

    def forward(ref, c):
        x = jnp.concatenate(
            [ref[pl.ds(c + n, LEN_A, stride=CH), :] for n in range(2)], axis=1
        )
        high, low = split(x)
        z = dot(first_ref[...], jnp.concatenate([high, low, high], axis=0))
        re, im = z[:64], z[64:]
        zr = re * cos_t + im * sin_t
        zi = im * cos_t - re * sin_t
        z = jnp.concatenate(
            [
                jnp.concatenate([zr[:, :128], zi[:, :128]], axis=1),
                jnp.concatenate([zr[:, 128:], zi[:, 128:]], axis=1),
            ],
            axis=0,
        )
        high, low = split(z)
        return dot(high, inner_ref[0]) + (dot(low, inner_ref[0]) + dot(high, inner_ref[1]))

    await_bytes(others(f_recv), recv_sem.at[1])
    await_bytes(others(r_recv), recv_sem.at[2])
    read_codes(f_recv, filter_t, 112)

    def filter_pair(m, carry):
        spec[pl.ds(pl.multiple_of(128 * m, 128), 128), :] = forward(filter_t, 2 * m)
        return carry

    lax.fori_loop(0, CH // 2, filter_pair, 0, unroll=2)

    def gather_four(i, total):
        blocks = r_recv[pl.ds(pl.multiple_of(4 * i, 4), 4)].reshape(4 * CH, 128)
        found = dot(blocks, onehot[...])
        for u in range(4):
            total = total + jnp.where(block_all == 4 * i + u, found[CH * u : CH * u + CH], 0.0)
        return total

    wanted = lax.fori_loop(0, N_CTX // 4, gather_four, jnp.zeros((CH, 1408), F32))
    for g in range(8):
        e_send[g] = wanted[:, 128 * g : 128 * g + 128].astype(BF16)
    send_ctx(4, lambda peer: e_send.at[peer // 4], e_recv)
    e_recv[me] = e_send[me // 4]
    q_end = (
        my_taps[:, 2:3] * wanted[:, 1024:1152]
        + my_taps[:, 1:2] * wanted[:, 1152:1280]
        + my_taps[:, 0:1] * wanted[:, 1280:1408]
    )

    await_bytes(others(s_recv), recv_sem.at[3])
    read_codes(s_recv, sig_t, 113)

    def convolve_pair(m, carry):
        x = forward(sig_t, 2 * m)
        f = spec[pl.ds(pl.multiple_of(128 * m, 128), 128), :]
        xr, xi, fr, fi = x[:, :128], x[:, 128:], f[:, :128], f[:, 128:]
        y = jnp.concatenate([xr * fr - xi * fi, xr * fi + xi * fr], axis=1)
        high, low = split(y)
        u = dot(high, inner_ref[2]) + (dot(low, inner_ref[2]) + dot(high, inner_ref[3]))
        ur = jnp.concatenate([u[:64, :128], u[64:, :128]], axis=1)
        ui = jnp.concatenate([u[:64, 128:], u[64:, 128:]], axis=1)
        w = jnp.concatenate([ur * cos_t - ui * sin_t, ui * cos_t + ur * sin_t], axis=0)
        high, low = split(w)
        y = dot(last_ref[...], jnp.concatenate([high, high], axis=0)) + dot(last_ref[:, :128], low)
        mixed[pl.ds(2 * m, LEN_A, stride=CH), :] = y[:, :128]
        mixed[pl.ds(2 * m + 1, LEN_A, stride=CH), :] = y[:, 128:]
        return carry

    lax.fori_loop(0, CH // 2, convolve_pair, 0, unroll=4)

    lane = iota((CH, 128), 1)
    end_half = t_end // 128
    end_spot = t_end - end_half * 128
    spot = jnp.where(iota((128, 128), 0) == end_spot, 1.0, 0.0).astype(BF16)
    spots = jnp.concatenate([spot, spot], axis=0)
    gain_col = my_taps[:, 9:10]
    gain_col = jnp.concatenate([gain_col, gain_col], axis=0)

    def finish_block(i, carry):
        ended, tiles = carry
        here = pl.ds(pl.multiple_of(i * 32, 32), 32)
        y = mixed[here, :]
        high, low = split(y + gain_col * sig_t[here, :])
        found = dot(jnp.concatenate([high, low], axis=1), spots)
        ended = ended + jnp.where(end_half == 2 * i, found[:CH], 0.0)
        ended = ended + jnp.where(end_half == 2 * i + 1, found[CH:], 0.0)
        step = row_scale(jnp.maximum(jnp.abs(y[:CH]), jnp.abs(y[CH:])), 1)
        both = jnp.concatenate([step, step], axis=0)
        m_send[i] = code(y * (1.0 / both))
        tiles = jnp.where(lane == 32 + i, step, tiles)
        return ended, tiles

    empty = jnp.zeros((CH, 128), F32)
    ended, tiles = lax.fori_loop(0, N_CTX, finish_block, (empty, empty), unroll=4)
    ended = q_end * ended
    for g in range(4):
        turned = pltpu.roll(ended, (128 - 32 * g) % 128, 1)
        moved = pltpu.roll(tiles, (128 - 8 * g) % 128, 1)
        l_send[g] = jnp.where(lane < 32, turned, moved).astype(BF16)
    send_ctx(5, lambda peer: l_send.at[peer // 8], l_recv)
    l_recv[me] = l_send[me // 8]
    send_ctx(6, lambda peer: m_send.at[peer], m_recv)
    m_recv[me] = m_send[me]

    def turn(received):
        tmp[...] = received[...].reshape(N_CTX * CH, 128).astype(F32).T

    await_bytes(others(e_recv), recv_sem.at[4])
    turn(e_recv)
    ge_recv[rep, ch] = tmp[pl.ds(pl.multiple_of(lax.rem(me, 4) * 32, 32), 32), :].astype(BF16)
    send_ch(7, ge_recv)

    await_bytes(others(l_recv), recv_sem.at[5])
    turn(l_recv)
    four = tmp[pl.ds(pl.multiple_of(my_z // 2 * 8, 8), 8), :]
    gl_recv[rep, ch] = jnp.where(lax.rem(my_z, 2) == 0, four[:4], four[4:])
    send_ch(8, gl_recv)
    scales = tmp[32:40, :]
    m_steps = jnp.sum(jnp.where(iota((8, 512), 0) == my_z, scales, 0.0), axis=0, keepdims=True)

    await_bytes(seven(ge_recv), recv_sem.at[7])
    swap_e = remote(9, ge_recv.at[rep], ge_recv.at[rep], sibling)
    swap_e.start()

    await_bytes(others(m_recv), recv_sem.at[6])
    gain = gain_ref[...]

    def gate(g):
        here = slice(128 * g, 128 * g + 128)
        for h in range(2):
            rows = slice(128 * h, 128 * h + 128)
            codes = decode(m_recv[8 * g : 8 * g + 8, CH * h : CH * h + CH, :]).reshape(128, 128)
            value = codes.T * m_steps[:, here]
            out_ref[rows, here] = (
                query[rows, here] * (value + gain[:, here] * signal[rows, here])
            ).astype(BF16)

    gate(0)
    gate(1)
    await_bytes(seven(gl_recv), recv_sem.at[8])
    swap_l = remote(10, gl_recv.at[rep], gl_recv.at[rep], sibling)
    swap_l.start()
    gate(2)
    gate(3)

    swap_e.wait_recv()
    for c in range(8):
        for r in range(2):
            lanes = slice(512 * (2 * c + r), 512 * (2 * c + r) + 512)
            rows = ge_recv[r, c].astype(F32)
            for k in range(6):
                states_ref[k, :, lanes] = rows[4 * k : 4 * k + 4].astype(BF16)
    swap_l.wait_recv()
    for c in range(8):
        for r in range(2):
            lanes = slice(512 * (2 * c + r), 512 * (2 * c + r) + 512)
            states_ref[6, :, lanes] = gl_recv[r, c].astype(BF16)

    halo_copy.wait_send()
    for n, buffer in ((1, f_recv), (2, r_recv), (3, s_recv), (4, e_recv), (5, l_recv), (6, m_recv)):
        await_bytes(others(buffer), send_sem.at[n])
    await_bytes(seven(ge_recv), send_sem.at[7])
    await_bytes(seven(gl_recv), send_sem.at[8])
    swap_e.wait_send()
    swap_l.wait_send()


def body(projections, short_taps, skip_gain, long_filter, request_ends, replica_of, slot_index):
    first, last, inner, turns = tables()
    whole = pl.BlockSpec(memory_space=pltpu.VMEM)
    operands = (
        projections, long_filter, short_taps, skip_gain.reshape(1, 512),
        request_ends.reshape(1, 128), replica_of.reshape(1, 128), slot_index.reshape(1, 128),
        jnp.asarray(first), jnp.asarray(last), jnp.asarray(inner), jnp.asarray(turns),
    )
    codes = pltpu.VMEM((N_CTX, 2 * CH, 128), jnp.int16)
    tiles = pltpu.VMEM((N_CTX, CH, 128), BF16)
    values = pltpu.VMEM((LEN_A * CH, 128), F32)
    tokens = pltpu.VMEM((TOK, 512), F32)
    output, states = pl.pallas_call(
        kernel,
        out_shape=(
            jax.ShapeDtypeStruct((TOK, 512), BF16),
            jax.ShapeDtypeStruct((7, SLOTS, 8192), BF16),
        ),
        in_specs=[pl.BlockSpec(memory_space=pltpu.HBM)] * len(operands),
        out_specs=(whole, whole),
        scratch_shapes=[
            *[pltpu.VMEM(x.shape, x.dtype) for x in operands],
            pltpu.VMEM((8, 512), F32), pltpu.VMEM((8, 512), F32),
            codes, codes, codes, tiles,
            pltpu.VMEM((8, CH, 128), BF16), pltpu.VMEM((4, CH, 128), BF16),
            codes, codes, codes, tiles, tiles, tiles,
            pltpu.VMEM((2, 8, 32, 512), BF16), pltpu.VMEM((2, 8, SLOTS, 512), F32),
            pltpu.VMEM((64 * CH, 256), F32),
            values, values, values, tokens, tokens,
            pltpu.VMEM((8, 512), F32),
            pltpu.VMEM((128, 1408), BF16),
            pltpu.VMEM((512, 16), F32),
            pltpu.VMEM((128, 512), F32),
            pltpu.SemaphoreType.DMA((11,)),
            pltpu.SemaphoreType.DMA((11,)),
            pltpu.SemaphoreType.DMA((11,)),
        ],
        compiler_params=pltpu.CompilerParams(
            collective_id=0, has_side_effects=True, vmem_limit_bytes=63 * 2**20
        ),
        cost_estimate=pl.CostEstimate(flops=2 * 10**9, bytes_accessed=4 * 10**6, transcendentals=0),
    )(*operands)
    return output, states.transpose(1, 0, 2)


def solution(mesh):
    return jax.shard_map(
        body,
        mesh=mesh,
        in_specs=(
            P(None, "ctx", ("ch", "rep")),
            P(None, None, ("ch", "rep")),
            P(("ch", "rep")),
            P("ctx", ("ch", "rep")),
            P(),
            P(),
            P(),
        ),
        out_specs=(P("ctx", ("ch", "rep")), P("ctx", None, None)),
        check_vma=False,
    )
```

time: 91.3 us -> 60.6 us (0.66)
  Pallas kernels: 80.1 us -> 57.3 us
  local copies, waits for them, and re-layouts: 10 us -> 2.49 us
    pallas_call x1, Pallas kernels: 80.1 us -> 57.3 us  [body(): pl.pallas_call(kernel, out_shape=(jax.ShapeDtypeStruct((TOK, 512), BF16),...]
    unnamed x25 -> x4, local copies, waits for them, and re-layouts: 8.87 us -> 2.49 us
    pallas_call x1 -> x0, local copies, waits for them, and re-layouts: 1.16 us -> none  [body(): pl.pallas_call(kernel, out_shape=(jax.ShapeDtypeStruct((TOK, 512), BF16),...]
where the time goes in v2:
time: 60.6 us; the launch traced here: 60.4 us
  Pallas kernels  57.3 us (95%)
  local copies, waits for them, and re-layouts  2.49 us (4%)
  between operations  0.65 us (1%)
    pallas_call x1, Pallas kernels, body(): pl.pallas_call(kernel, out_shape=(jax.ShapeDtypeStruct((TOK, 512), BF16),...  57.3 us
    unnamed x4, local copies, waits for them, and re-layouts  2.49 us

profile of v2, /device:TPU:1, one launch (start us, length us, event | category | flops | bytes accessed | tf_op | source)
XLA Modules:
  0.0 60.4 jit_solution(11255536838187662818)
XLA Ops:
  0.6 57.3 %shard_map.122 = (bf16[256,512]{1,0:T(8,128)(2,1)}, bf16[7,4,8192]{2,1,0:T(4,128)(2,1)}) custom-call(bf16[3,256,512]{2,1,0:T(8,128)(2,1)} %refs_0_.1, f32[256,512]{1,0:T(8,128)} %refs_1_.1, f32[3,3,512]{2,1,0:T(4,128)} %refs_2_.1, f32[1,512]{1,0:T(1,128)} %bitcast.6, s32[1,128]{1,0:T(1,128)} %bitcast.7, s32[1,128]{1,0:T(1,128)} %bitcast.8, ...), custom_call_target="tpu_custom_call" | custom-call | flops 2000000000 | bytes 4000000 | tf_op jit(solution)/shard_map/pallas_call | solution.py:461
  57.9 0.0 copy-start
  57.9 1.7 %copy.15 = bf16[256,512]{1,0:T(8,128)(2,1)} copy(bf16[256,512]{1,0:T(8,128)(2,1)} %get-tuple-element.8) | data formatting | bytes 524288
  59.6 0.0 copy-done
  59.6 0.8 %copy.16 = bf16[4,7,8192]{2,0,1:T(4,128)(2,1)} copy(bf16[4,7,8192]{2,0,1:T(4,128)(2,1)S(1)} %bitcast.5) | data formatting | bytes 917504
Async XLA Ops:
  57.9 1.7 %copy-start = (bf16[7,4,8192]{2,1,0:T(4,128)(2,1)S(1)}, bf16[7,4,8192]{2,1,0:T(4,128)(2,1)}, u32[]{:S(2)}) copy-start(bf16[7,4,8192]{2,1,0:T(4,128)(2,1)} %get-tuple-element.5) | copy-start | bytes 1376260

commit v3 on v2

--- a/solution.py
+++ b/solution.py
@@ -82,7 +82,7 @@
         first_ref, last_ref, inner_ref, turns_ref,
     ) = vmem_refs
     (
-        halo_send, halo_recv, f_send, s_send, m_send, r_send, e_send, l_send,
+        halo_send, halo_recv, step_send, step_recv, f_send, s_send, m_send, r_send, e_send, l_send,
         f_recv, s_recv, m_recv, r_recv, e_recv, l_recv, ge_recv, gl_recv,
         spec, filter_t, sig_t, mixed, query, signal, steps, onehot, taps_t, tmp,
         local_sem, send_sem, recv_sem,
@@ -109,13 +109,18 @@
         greet({"ctx": lax.rem(me + t, N_CTX)})
         return carry
 
-    def greet_ch(t, carry):
-        greet({"ch": lax.rem(ch + t, 8)})
+    mine_near = ch * 2 + rep
+
+    def near(t):
+        other = lax.rem(mine_near + t, 16)
+        return {"ch": other // 2, "rep": lax.rem(other, 2)}
+
+    def greet_near(t, carry):
+        greet(near(t))
         return carry
 
     lax.fori_loop(1, N_CTX, greet_ctx, 0)
-    lax.fori_loop(1, 8, greet_ch, 0)
-    greet(sibling)
+    lax.fori_loop(1, 16, greet_near, 0)
 
     def remote(n, source, target, device):
         return pltpu.make_async_remote_copy(
@@ -145,6 +150,13 @@
 
         lax.fori_loop(1, 8, one, 0)
 
+    def send_near(n, buffer):
+        def one(t, carry):
+            remote(n, buffer.at[mine_near], buffer.at[mine_near], near(t)).start()
+            return carry
+
+        lax.fori_loop(1, 16, one, 0)
+
     def await_bytes(part, sem):
         pltpu.make_async_copy(part, part, sem).wait()
 
@@ -162,14 +174,16 @@
         devices, lanes = column_block(dx)
         step = row_scale(block, 0)
         steps[kind : kind + 1, lanes] = step
-        turned = (block * (1.0 / step)).T
-        for h in range(2):
-            target[devices, CH * h : CH * h + CH] = code(
-                turned[:, 128 * h : 128 * h + 128]
-            ).reshape(8, CH, 128)
+        turned = (block * (1.0 / step)).T.reshape(8, CH, TOK)
+        parts = [
+            turned[:, 8 * q : 8 * q + 8, 128 * h : 128 * h + 128] for q in range(2) for h in range(2)
+        ]
+        target[devices] = code(jnp.concatenate(parts, axis=1))
 
     def put_filter(dx):
-        put_codes(filt[:, column_block(dx)[1]], 0, dx, f_send)
+        lanes = column_block(dx)[1]
+        put_codes(filt[:, lanes], 0, dx, f_send)
+        step_send[lax.rem(my_x + dx, 4)] = steps[0:1, lanes]
 
     loads[0].wait()
     halo_send[...] = jnp.concatenate(
@@ -178,14 +192,16 @@
     steps[...] = jnp.zeros((8, 512), F32)
     loads[1].wait()
     put_filter(0)
-    pl.semaphore_wait(barrier, N_CTX - 1 + 7 + 1)
+    pl.semaphore_wait(barrier, N_CTX - 1 + 15)
     halo_copy = remote(0, halo_send, halo_recv, after)
     halo_copy.start()
     for dx in range(4):
         if dx > 0:
             put_filter(dx)
         send_line(1, lambda peer: f_send.at[peer], f_recv, dx)
+        send_line(9, lambda peer: step_send.at[peer // 8], step_recv, dx)
     f_recv[me] = f_send[me]
+    step_recv[me] = step_send[me // 8]
     for load in loads[2:]:
         load.wait()
 
@@ -263,7 +279,21 @@
         r_send[devices] = rows.T.astype(BF16).reshape(8, CH, 128)
         send_line(2, lambda peer: r_send.at[peer], r_recv, dx)
     r_recv[me] = r_send[me]
-    send_ctx(3, lambda peer: s_send.at[peer], s_recv)
+    half = [pl.ds(CH * q, CH) for q in range(2)]
+
+    def send_half(n, q, source, target):
+        for dx in range(4):
+            x = lax.rem(my_x + dx, 4)
+
+            def one(t, carry):
+                peer = 8 * x + lax.rem(my_z + t, 8)
+                remote(n, source.at[peer, half[q]], target.at[me, half[q]], {"ctx": peer}).start()
+                return carry
+
+            lax.fori_loop(1 if dx == 0 else 0, 8, one, 0)
+
+    send_half(3, 0, s_send, s_recv)
+    send_half(10, 1, s_send, s_recv)
     s_recv[me] = s_send[me]
 
     rows = [taps_ref[p] for p in range(3)] + [gain_ref[...], jnp.zeros((6, 512), F32)]
@@ -272,44 +302,35 @@
 
     cos_t, sin_t = turns_ref[0], turns_ref[1]
 
-    def read_codes(received, target, lane):
-        def one(i, carry):
-            step = r_recv[i].astype(F32)[:, lane : lane + 1]
+    def read_codes(received, q, step_of, target):
+        for i in range(N_CTX):
+            step = step_of(i)[8 * q : 8 * q + 8]
             step = jnp.concatenate([step, step], axis=0)
-            target[pl.ds(pl.multiple_of(i * 32, 32), 32), :] = decode(received[i]) * step
-            return carry
-
-        lax.fori_loop(0, N_CTX, one, 0, unroll=4)
-
-    def forward(ref, c):
-        x = jnp.concatenate(
-            [ref[pl.ds(c + n, LEN_A, stride=CH), :] for n in range(2)], axis=1
-        )
-        high, low = split(x)
-        z = dot(first_ref[...], jnp.concatenate([high, low, high], axis=0))
-        re, im = z[:64], z[64:]
-        zr = re * cos_t + im * sin_t
-        zi = im * cos_t - re * sin_t
-        z = jnp.concatenate(
-            [
-                jnp.concatenate([zr[:, :128], zi[:, :128]], axis=1),
-                jnp.concatenate([zr[:, 128:], zi[:, 128:]], axis=1),
-            ],
-            axis=0,
-        )
-        high, low = split(z)
+            target[q, 16 * i : 16 * i + 16, :] = decode(received[i, CH * q : CH * q + CH, :]) * step
+
+    def forward(ref):
+        turned = []
+        for c in range(0, 8, 2):
+            x = jnp.concatenate([ref[pl.ds(c + n, LEN_A, stride=8), :] for n in range(2)], axis=1)
+            high, low = split(x)
+            z = dot(first_ref[...], jnp.concatenate([high, low, high], axis=0))
+            re, im = z[:64], z[64:]
+            zr = re * cos_t + im * sin_t
+            zi = im * cos_t - re * sin_t
+            for n in (slice(0, 128), slice(128, 256)):
+                turned.append(jnp.concatenate([zr[:, n], zi[:, n]], axis=1))
+        high, low = split(jnp.concatenate(turned, axis=0))
         return dot(high, inner_ref[0]) + (dot(low, inner_ref[0]) + dot(high, inner_ref[1]))
 
     await_bytes(others(f_recv), recv_sem.at[1])
+    await_bytes(others(step_recv), recv_sem.at[9])
+    tmp[:, :32] = step_recv[...].reshape(N_CTX, 128).T
+    f_steps = tmp[pl.ds(pl.multiple_of(my_z * CH, CH), CH), :32]
+    for q in range(2):
+        read_codes(f_recv, q, lambda i: f_steps[:, i : i + 1], filter_t)
+        spec[q] = forward(filter_t.at[q])
+
     await_bytes(others(r_recv), recv_sem.at[2])
-    read_codes(f_recv, filter_t, 112)
-
-    def filter_pair(m, carry):
-        spec[pl.ds(pl.multiple_of(128 * m, 128), 128), :] = forward(filter_t, 2 * m)
-        return carry
-
-    lax.fori_loop(0, CH // 2, filter_pair, 0, unroll=2)
-
     def gather_four(i, total):
         blocks = r_recv[pl.ds(pl.multiple_of(4 * i, 4), 4)].reshape(4 * CH, 128)
         found = dot(blocks, onehot[...])
@@ -328,101 +349,107 @@
         + my_taps[:, 0:1] * wanted[:, 1280:1408]
     )
 
-    await_bytes(others(s_recv), recv_sem.at[3])
-    read_codes(s_recv, sig_t, 113)
-
-    def convolve_pair(m, carry):
-        x = forward(sig_t, 2 * m)
-        f = spec[pl.ds(pl.multiple_of(128 * m, 128), 128), :]
+    lane = iota((8, 128), 1)
+    end_half = t_end // 128
+    end_spot = t_end - end_half * 128
+    spot = jnp.where(iota((128, 128), 0) == end_spot, 1.0, 0.0).astype(BF16)
+    spots = jnp.concatenate([spot, spot], axis=0)
+
+    def convolve(q):
+        read_codes(s_recv, q, lambda i: r_recv[i].astype(F32)[:, 113:114], sig_t)
+        x, f = forward(sig_t.at[q]), spec[q]
         xr, xi, fr, fi = x[:, :128], x[:, 128:], f[:, :128], f[:, 128:]
         y = jnp.concatenate([xr * fr - xi * fi, xr * fi + xi * fr], axis=1)
         high, low = split(y)
         u = dot(high, inner_ref[2]) + (dot(low, inner_ref[2]) + dot(high, inner_ref[3]))
-        ur = jnp.concatenate([u[:64, :128], u[64:, :128]], axis=1)
-        ui = jnp.concatenate([u[:64, 128:], u[64:, 128:]], axis=1)
-        w = jnp.concatenate([ur * cos_t - ui * sin_t, ui * cos_t + ur * sin_t], axis=0)
-        high, low = split(w)
-        y = dot(last_ref[...], jnp.concatenate([high, high], axis=0)) + dot(last_ref[:, :128], low)
-        mixed[pl.ds(2 * m, LEN_A, stride=CH), :] = y[:, :128]
-        mixed[pl.ds(2 * m + 1, LEN_A, stride=CH), :] = y[:, 128:]
-        return carry
-
-    lax.fori_loop(0, CH // 2, convolve_pair, 0, unroll=4)
-
+        for c in range(0, 8, 2):
+            one, two = u[64 * c : 64 * c + 64], u[64 * c + 64 : 64 * c + 128]
+            ur = jnp.concatenate([one[:, :128], two[:, :128]], axis=1)
+            ui = jnp.concatenate([one[:, 128:], two[:, 128:]], axis=1)
+            w = jnp.concatenate([ur * cos_t - ui * sin_t, ui * cos_t + ur * sin_t], axis=0)
+            high, low = split(w)
+            y = dot(last_ref[...], jnp.concatenate([high, high], axis=0)) + dot(last_ref[:, :128], low)
+            mixed[pl.ds(c, LEN_A, stride=8), :] = y[:, :128]
+            mixed[pl.ds(c + 1, LEN_A, stride=8), :] = y[:, 128:]
+
+    def put_mixed(q):
+        gain_col = my_taps[8 * q : 8 * q + 8, 9:10]
+        gain_col = jnp.concatenate([gain_col] * 8, axis=0)
+
+        def four_blocks(j, carry):
+            ended, tiles = carry
+            here = pl.ds(pl.multiple_of(j * 64, 64), 64)
+            y = mixed[here, :]
+            high, low = split(y + gain_col * sig_t[q, here, :])
+            found = dot(jnp.concatenate([high, low], axis=1), spots)
+            for u in range(8):
+                ended = ended + jnp.where(end_half == 8 * j + u, found[8 * u : 8 * u + 8], 0.0)
+            for u in range(4):
+                block = y[16 * u : 16 * u + 16]
+                step = row_scale(jnp.maximum(jnp.abs(block[:8]), jnp.abs(block[8:])), 1)
+                both = jnp.concatenate([step, step], axis=0)
+                m_send[4 * j + u, CH * q : CH * q + CH] = code(block * (1.0 / both))
+                tiles = jnp.where(lane == 32 + 4 * j + u, step, tiles)
+            return ended, tiles
+
+        empty = jnp.zeros((8, 128), F32)
+        return lax.fori_loop(0, N_CTX // 4, four_blocks, (empty, empty), unroll=2)
+
+    def turn(received):
+        tmp[...] = received[...].reshape(N_CTX * CH, 128).astype(F32).T
+
+    await_bytes(s_recv.at[pl.ds(0, N_CTX - 1), half[0]], recv_sem.at[3])
+    convolve(0)
+    ended0, tiles0 = put_mixed(0)
+    send_half(6, 0, m_send, m_recv)
+
+    await_bytes(s_recv.at[pl.ds(0, N_CTX - 1), half[1]], recv_sem.at[10])
+    convolve(1)
+    ended1, tiles1 = put_mixed(1)
+    ended = q_end * jnp.concatenate([ended0, ended1], axis=0)
+    tiles = jnp.concatenate([tiles0, tiles1], axis=0)
     lane = iota((CH, 128), 1)
-    end_half = t_end // 128
-    end_spot = t_end - end_half * 128
-    spot = jnp.where(iota((128, 128), 0) == end_spot, 1.0, 0.0).astype(BF16)
-    spots = jnp.concatenate([spot, spot], axis=0)
-    gain_col = my_taps[:, 9:10]
-    gain_col = jnp.concatenate([gain_col, gain_col], axis=0)
-
-    def finish_block(i, carry):
-        ended, tiles = carry
-        here = pl.ds(pl.multiple_of(i * 32, 32), 32)
-        y = mixed[here, :]
-        high, low = split(y + gain_col * sig_t[here, :])
-        found = dot(jnp.concatenate([high, low], axis=1), spots)
-        ended = ended + jnp.where(end_half == 2 * i, found[:CH], 0.0)
-        ended = ended + jnp.where(end_half == 2 * i + 1, found[CH:], 0.0)
-        step = row_scale(jnp.maximum(jnp.abs(y[:CH]), jnp.abs(y[CH:])), 1)
-        both = jnp.concatenate([step, step], axis=0)
-        m_send[i] = code(y * (1.0 / both))
-        tiles = jnp.where(lane == 32 + i, step, tiles)
-        return ended, tiles
-
-    empty = jnp.zeros((CH, 128), F32)
-    ended, tiles = lax.fori_loop(0, N_CTX, finish_block, (empty, empty), unroll=4)
-    ended = q_end * ended
     for g in range(4):
         turned = pltpu.roll(ended, (128 - 32 * g) % 128, 1)
         moved = pltpu.roll(tiles, (128 - 8 * g) % 128, 1)
         l_send[g] = jnp.where(lane < 32, turned, moved).astype(BF16)
     send_ctx(5, lambda peer: l_send.at[peer // 8], l_recv)
     l_recv[me] = l_send[me // 8]
-    send_ctx(6, lambda peer: m_send.at[peer], m_recv)
-    m_recv[me] = m_send[me]
-
-    def turn(received):
-        tmp[...] = received[...].reshape(N_CTX * CH, 128).astype(F32).T
 
     await_bytes(others(e_recv), recv_sem.at[4])
     turn(e_recv)
     ge_recv[rep, ch] = tmp[pl.ds(pl.multiple_of(lax.rem(me, 4) * 32, 32), 32), :].astype(BF16)
     send_ch(7, ge_recv)
 
+    send_half(11, 1, m_send, m_recv)
+    m_recv[me] = m_send[me]
+
+    await_bytes(seven(ge_recv), recv_sem.at[7])
+    swap_e = remote(12, ge_recv.at[rep], ge_recv.at[rep], sibling)
+    swap_e.start()
+
     await_bytes(others(l_recv), recv_sem.at[5])
     turn(l_recv)
     four = tmp[pl.ds(pl.multiple_of(my_z // 2 * 8, 8), 8), :]
-    gl_recv[rep, ch] = jnp.where(lax.rem(my_z, 2) == 0, four[:4], four[4:])
-    send_ch(8, gl_recv)
+    gl_recv[mine_near] = jnp.where(lax.rem(my_z, 2) == 0, four[:4], four[4:])
+    send_near(8, gl_recv)
     scales = tmp[32:40, :]
     m_steps = jnp.sum(jnp.where(iota((8, 512), 0) == my_z, scales, 0.0), axis=0, keepdims=True)
 
-    await_bytes(seven(ge_recv), recv_sem.at[7])
-    swap_e = remote(9, ge_recv.at[rep], ge_recv.at[rep], sibling)
-    swap_e.start()
-
-    await_bytes(others(m_recv), recv_sem.at[6])
+    await_bytes(m_recv.at[pl.ds(0, N_CTX - 1), half[0]], recv_sem.at[6])
+    await_bytes(m_recv.at[pl.ds(0, N_CTX - 1), half[1]], recv_sem.at[11])
     gain = gain_ref[...]
 
-    def gate(g):
+    for g in range(4):
         here = slice(128 * g, 128 * g + 128)
+        codes = decode(m_recv[8 * g : 8 * g + 8])
         for h in range(2):
             rows = slice(128 * h, 128 * h + 128)
-            codes = decode(m_recv[8 * g : 8 * g + 8, CH * h : CH * h + CH, :]).reshape(128, 128)
-            value = codes.T * m_steps[:, here]
+            parts = [codes[:, CH * q + 8 * h : CH * q + 8 * h + 8] for q in range(2)]
+            value = jnp.concatenate(parts, axis=1).reshape(128, 128).T * m_steps[:, here]
             out_ref[rows, here] = (
                 query[rows, here] * (value + gain[:, here] * signal[rows, here])
             ).astype(BF16)
-
-    gate(0)
-    gate(1)
-    await_bytes(seven(gl_recv), recv_sem.at[8])
-    swap_l = remote(10, gl_recv.at[rep], gl_recv.at[rep], sibling)
-    swap_l.start()
-    gate(2)
-    gate(3)
 
     swap_e.wait_recv()
     for c in range(8):
@@ -431,19 +458,18 @@
             rows = ge_recv[r, c].astype(F32)
             for k in range(6):
                 states_ref[k, :, lanes] = rows[4 * k : 4 * k + 4].astype(BF16)
-    swap_l.wait_recv()
-    for c in range(8):
-        for r in range(2):
-            lanes = slice(512 * (2 * c + r), 512 * (2 * c + r) + 512)
-            states_ref[6, :, lanes] = gl_recv[r, c].astype(BF16)
+    await_bytes(gl_recv.at[pl.ds(0, 15)], recv_sem.at[8])
+    for j in range(16):
+        states_ref[6, :, 512 * j : 512 * j + 512] = gl_recv[j].astype(BF16)
 
     halo_copy.wait_send()
-    for n, buffer in ((1, f_recv), (2, r_recv), (3, s_recv), (4, e_recv), (5, l_recv), (6, m_recv)):
+    for n, buffer in ((1, f_recv), (2, r_recv), (4, e_recv), (5, l_recv), (9, step_recv)):
         await_bytes(others(buffer), send_sem.at[n])
+    for n, buffer in ((3, s_recv), (6, m_recv), (10, s_recv), (11, m_recv)):
+        await_bytes(buffer.at[pl.ds(0, N_CTX - 1), half[0]], send_sem.at[n])
     await_bytes(seven(ge_recv), send_sem.at[7])
-    await_bytes(seven(gl_recv), send_sem.at[8])
+    await_bytes(gl_recv.at[pl.ds(0, 15)], send_sem.at[8])
     swap_e.wait_send()
-    swap_l.wait_send()
 
 
 def body(projections, short_taps, skip_gain, long_filter, request_ends, replica_of, slot_index):
@@ -456,7 +482,7 @@
     )
     codes = pltpu.VMEM((N_CTX, 2 * CH, 128), jnp.int16)
     tiles = pltpu.VMEM((N_CTX, CH, 128), BF16)
-    values = pltpu.VMEM((LEN_A * CH, 128), F32)
+    values = pltpu.VMEM((2, 512, 128), F32)
     tokens = pltpu.VMEM((TOK, 512), F32)
     output, states = pl.pallas_call(
         kernel,
@@ -469,19 +495,20 @@
         scratch_shapes=[
             *[pltpu.VMEM(x.shape, x.dtype) for x in operands],
             pltpu.VMEM((8, 512), F32), pltpu.VMEM((8, 512), F32),
+            pltpu.VMEM((4, 1, 128), F32), pltpu.VMEM((N_CTX, 1, 128), F32),
             codes, codes, codes, tiles,
             pltpu.VMEM((8, CH, 128), BF16), pltpu.VMEM((4, CH, 128), BF16),
             codes, codes, codes, tiles, tiles, tiles,
-            pltpu.VMEM((2, 8, 32, 512), BF16), pltpu.VMEM((2, 8, SLOTS, 512), F32),
-            pltpu.VMEM((64 * CH, 256), F32),
-            values, values, values, tokens, tokens,
+            pltpu.VMEM((2, 8, 32, 512), BF16), pltpu.VMEM((16, SLOTS, 512), F32),
+            pltpu.VMEM((2, 512, 256), F32),
+            values, values, pltpu.VMEM((512, 128), F32), tokens, tokens,
             pltpu.VMEM((8, 512), F32),
             pltpu.VMEM((128, 1408), BF16),
             pltpu.VMEM((512, 16), F32),
             pltpu.VMEM((128, 512), F32),
             pltpu.SemaphoreType.DMA((11,)),
-            pltpu.SemaphoreType.DMA((11,)),
-            pltpu.SemaphoreType.DMA((11,)),
+            pltpu.SemaphoreType.DMA((13,)),
+            pltpu.SemaphoreType.DMA((13,)),
         ],
         compiler_params=pltpu.CompilerParams(
             collective_id=0, has_side_effects=True, vmem_limit_bytes=63 * 2**20

time: 60.6 us -> 56.6 us (0.934)
  Pallas kernels: 57.3 us -> 53.3 us
    pallas_call x1, Pallas kernels: 57.3 us -> 53.3 us  [body(): pl.pallas_call(kernel, out_shape=(jax.ShapeDtypeStruct((TOK, 512), BF16),...]
where the time goes in v3:
time: 56.6 us; the launch traced here: 56.5 us
  Pallas kernels  53.3 us (94%)
  local copies, waits for them, and re-layouts  2.49 us (4%)
  between operations  0.65 us (1%)
    pallas_call x1, Pallas kernels, body(): pl.pallas_call(kernel, out_shape=(jax.ShapeDtypeStruct((TOK, 512), BF16),...  53.3 us
    unnamed x4, local copies, waits for them, and re-layouts  2.49 us

profile of v3, /device:TPU:1, one launch (start us, length us, event | category | flops | bytes accessed | tf_op | source)
XLA Modules:
  0.0 56.5 jit_solution(6132259266743720855)
XLA Ops:
  0.6 53.3 %shard_map.122 = (bf16[256,512]{1,0:T(8,128)(2,1)}, bf16[7,4,8192]{2,1,0:T(4,128)(2,1)}) custom-call(bf16[3,256,512]{2,1,0:T(8,128)(2,1)} %refs_0_.1, f32[256,512]{1,0:T(8,128)} %refs_1_.1, f32[3,3,512]{2,1,0:T(4,128)} %refs_2_.1, f32[1,512]{1,0:T(1,128)} %bitcast.6, s32[1,128]{1,0:T(1,128)} %bitcast.7, s32[1,128]{1,0:T(1,128)} %bitcast.8, ...), custom_call_target="tpu_custom_call" | custom-call | flops 2000000000 | bytes 4000000 | tf_op jit(solution)/shard_map/pallas_call | solution.py:487
  54.0 0.0 copy-start
  54.0 1.7 %copy.15 = bf16[256,512]{1,0:T(8,128)(2,1)} copy(bf16[256,512]{1,0:T(8,128)(2,1)} %get-tuple-element.8) | data formatting | bytes 524288
  55.7 0.0 copy-done
  55.7 0.8 %copy.16 = bf16[4,7,8192]{2,0,1:T(4,128)(2,1)} copy(bf16[4,7,8192]{2,0,1:T(4,128)(2,1)S(1)} %bitcast.5) | data formatting | bytes 917504
Async XLA Ops:
  54.0 1.7 %copy-start = (bf16[7,4,8192]{2,1,0:T(4,128)(2,1)S(1)}, bf16[7,4,8192]{2,1,0:T(4,128)(2,1)}, u32[]{:S(2)}) copy-start(bf16[7,4,8192]{2,1,0:T(4,128)(2,1)} %get-tuple-element.5) | copy-start | bytes 1376260

commit v4 on v3

--- a/solution.py
+++ b/solution.py
@@ -431,7 +431,10 @@
     await_bytes(others(l_recv), recv_sem.at[5])
     turn(l_recv)
     four = tmp[pl.ds(pl.multiple_of(my_z // 2 * 8, 8), 8), :]
-    gl_recv[mine_near] = jnp.where(lax.rem(my_z, 2) == 0, four[:4], four[4:])
+    four = jnp.where(lax.rem(my_z, 2) == 0, four[:4], four[4:])
+    gl_recv[mine_near] = jnp.concatenate(
+        [four[:, 128 * g : 128 * g + 128] for g in range(4)], axis=0
+    ).astype(BF16)
     send_near(8, gl_recv)
     scales = tmp[32:40, :]
     m_steps = jnp.sum(jnp.where(iota((8, 512), 0) == my_z, scales, 0.0), axis=0, keepdims=True)
@@ -460,7 +463,10 @@
                 states_ref[k, :, lanes] = rows[4 * k : 4 * k + 4].astype(BF16)
     await_bytes(gl_recv.at[pl.ds(0, 15)], recv_sem.at[8])
     for j in range(16):
-        states_ref[6, :, 512 * j : 512 * j + 512] = gl_recv[j].astype(BF16)
+        rows = gl_recv[j].astype(F32)
+        for g in range(4):
+            first_lane = 512 * j + 128 * g
+            states_ref[6, :, first_lane : first_lane + 128] = rows[4 * g : 4 * g + 4].astype(BF16)
 
     halo_copy.wait_send()
     for n, buffer in ((1, f_recv), (2, r_recv), (4, e_recv), (5, l_recv), (9, step_recv)):
@@ -487,8 +493,8 @@
     output, states = pl.pallas_call(
         kernel,
         out_shape=(
-            jax.ShapeDtypeStruct((TOK, 512), BF16),
-            jax.ShapeDtypeStruct((7, SLOTS, 8192), BF16),
+            pltpu.VMEM((TOK, 512), BF16),
+            pltpu.VMEM((7, SLOTS, 8192), BF16),
         ),
         in_specs=[pl.BlockSpec(memory_space=pltpu.HBM)] * len(operands),
         out_specs=(whole, whole),
@@ -499,7 +505,7 @@
             codes, codes, codes, tiles,
             pltpu.VMEM((8, CH, 128), BF16), pltpu.VMEM((4, CH, 128), BF16),
             codes, codes, codes, tiles, tiles, tiles,
-            pltpu.VMEM((2, 8, 32, 512), BF16), pltpu.VMEM((16, SLOTS, 512), F32),
+            pltpu.VMEM((2, 8, 32, 512), BF16), pltpu.VMEM((16, 16, 128), BF16),
             pltpu.VMEM((2, 512, 256), F32),
             values, values, pltpu.VMEM((512, 128), F32), tokens, tokens,
             pltpu.VMEM((8, 512), F32),

time: 56.6 us -> 53.9 us (0.952)
  Pallas kernels: 53.3 us -> 51.7 us
  local copies, waits for them, and re-layouts: 2.49 us -> 1.47 us
    pallas_call x1, Pallas kernels: 53.3 us -> 51.7 us  [body(): pl.pallas_call(kernel, out_shape=(pltpu.VMEM((TOK, 512), BF16), pltpu.VME...]
    unnamed x4 -> x2, local copies, waits for them, and re-layouts: 2.49 us -> 1.47 us
where the time goes in v4:
time: 53.9 us; the launch traced here: 53.8 us
  Pallas kernels  51.7 us (96%)
  local copies, waits for them, and re-layouts  1.47 us (3%)
  between operations  0.64 us (1%)
    pallas_call x1, Pallas kernels, body(): pl.pallas_call(kernel, out_shape=(pltpu.VMEM((TOK, 512), BF16), pltpu.VME...  51.7 us
    unnamed x2, local copies, waits for them, and re-layouts  1.47 us

profile of v4, /device:TPU:1, one launch (start us, length us, event | category | flops | bytes accessed | tf_op | source)
XLA Modules:
  0.0 53.8 jit_solution(190575663265903886)
XLA Ops:
  0.6 51.7 %shard_map.122 = (bf16[256,512]{1,0:T(8,128)(2,1)S(1)}, bf16[7,4,8192]{2,1,0:T(4,128)(2,1)S(1)}) custom-call(bf16[3,256,512]{2,1,0:T(8,128)(2,1)} %refs_0_.1, f32[256,512]{1,0:T(8,128)} %refs_1_.1, f32[3,3,512]{2,1,0:T(4,128)} %refs_2_.1, f32[1,512]{1,0:T(1,128)} %bitcast.6, s32[1,128]{1,0:T(1,128)} %bitcast.7, s32[1,128]{1,0:T(1,128)} %bitcast.8, ...), custom_call_target="tpu_custom_call" | custom-call | flops 2000000000 | bytes 4000000 | tf_op jit(solution)/shard_map/pallas_call | solution.py:493
  52.3 0.7 %copy.15 = bf16[256,512]{1,0:T(8,128)(2,1)} copy(bf16[256,512]{1,0:T(8,128)(2,1)S(1)} %get-tuple-element.6) | data formatting | bytes 524288
  53.0 0.8 %copy.16 = bf16[4,7,8192]{2,0,1:T(4,128)(2,1)} copy(bf16[4,7,8192]{2,0,1:T(4,128)(2,1)S(1)} %bitcast.5) | data formatting | bytes 917504

commit v5 on v4

--- a/solution.py
+++ b/solution.py
@@ -424,10 +424,6 @@
     send_half(11, 1, m_send, m_recv)
     m_recv[me] = m_send[me]
 
-    await_bytes(seven(ge_recv), recv_sem.at[7])
-    swap_e = remote(12, ge_recv.at[rep], ge_recv.at[rep], sibling)
-    swap_e.start()
-
     await_bytes(others(l_recv), recv_sem.at[5])
     turn(l_recv)
     four = tmp[pl.ds(pl.multiple_of(my_z // 2 * 8, 8), 8), :]
@@ -436,6 +432,11 @@
         [four[:, 128 * g : 128 * g + 128] for g in range(4)], axis=0
     ).astype(BF16)
     send_near(8, gl_recv)
+
+    await_bytes(seven(ge_recv), recv_sem.at[7])
+    swap_e = remote(12, ge_recv.at[rep], ge_recv.at[rep], sibling)
+    swap_e.start()
+
     scales = tmp[32:40, :]
     m_steps = jnp.sum(jnp.where(iota((8, 512), 0) == my_z, scales, 0.0), axis=0, keepdims=True)
 

time: 53.9 us -> 53.9 us (level)
  no operation moved by 1% of the time
where the time goes in v5:
time: 53.9 us; the launch traced here: 53.8 us
  Pallas kernels  51.7 us (96%)
  local copies, waits for them, and re-layouts  1.47 us (3%)
  between operations  0.64 us (1%)
    pallas_call x1, Pallas kernels, body(): pl.pallas_call(kernel, out_shape=(pltpu.VMEM((TOK, 512), BF16), pltpu.VME...  51.7 us
    unnamed x2, local copies, waits for them, and re-layouts  1.47 us

profile of v5, /device:TPU:1, one launch (start us, length us, event | category | flops | bytes accessed | tf_op | source)
XLA Modules:
  0.0 53.8 jit_solution(11876248230931286774)
XLA Ops:
  0.6 51.7 %shard_map.122 = (bf16[256,512]{1,0:T(8,128)(2,1)S(1)}, bf16[7,4,8192]{2,1,0:T(4,128)(2,1)S(1)}) custom-call(bf16[3,256,512]{2,1,0:T(8,128)(2,1)} %refs_0_.1, f32[256,512]{1,0:T(8,128)} %refs_1_.1, f32[3,3,512]{2,1,0:T(4,128)} %refs_2_.1, f32[1,512]{1,0:T(1,128)} %bitcast.6, s32[1,128]{1,0:T(1,128)} %bitcast.7, s32[1,128]{1,0:T(1,128)} %bitcast.8, ...), custom_call_target="tpu_custom_call" | custom-call | flops 2000000000 | bytes 4000000 | tf_op jit(solution)/shard_map/pallas_call | solution.py:494
  52.3 0.7 %copy.15 = bf16[256,512]{1,0:T(8,128)(2,1)} copy(bf16[256,512]{1,0:T(8,128)(2,1)S(1)} %get-tuple-element.6) | data formatting | bytes 524288
  53.0 0.8 %copy.16 = bf16[4,7,8192]{2,0,1:T(4,128)(2,1)} copy(bf16[4,7,8192]{2,0,1:T(4,128)(2,1)S(1)} %bitcast.5) | data formatting | bytes 917504
